TPU v7x, 32 devices: a whole 2x2x4 slice. The times are simulated.
32 devices in a mesh: dp: 16 (over z, x, core), mp: 2 (over y).
Axes of the slice: x: 2, y: 2, z: 4, core: 2. Of those that a mesh axis runs over, the one named last changes fastest.
Arguments:
- kernel_state: float32 [3, 1024, 2304], P(None, 'mp'), may hold values from -2 to 2, as said below
- qkv_state: float32 [3, 768, 2304], P(None, 'dp', 'mp'), may hold values from -2 to 2, as said below
- proj_state: float32 [3, 768, 768], P(None, 'dp', 'mp'), may hold values from -4 to 4, as said below
- fc1_state: float32 [3, 768, 3072], P(None, 'dp', 'mp'), may hold values from -2 to 2, as said below
- fc2_state: float32 [3, 3072, 768], P(None, 'dp', 'mp'), may hold values from -2 to 2, as said below
- table_state: float32 [3, 60, 768], replicated, may hold values from -4 to 8, as said below
- patches_s: bfloat16 [32, 784, 192], P('dp'), may hold values from -6 to 6
- patches_l: bfloat16 [64, 16, 6912], P('dp'), may hold values from -6 to 6
- resize_s: float32 [64, 1024], P(None, 'mp'), may hold values from -2 to 2
- resize_l: float32 [2304, 1024], P(None, 'mp'), may hold values from -0.3125 to 0.3125
- bilin_s: float32 [784, 49], replicated, may hold values from 0 to 0.040816326
- bilin_l: float32 [16, 49], replicated, may hold values from 0 to 0.040816326
- cotangent: float32 [26112, 768], P(('dp', 'mp')), may hold values from -6 to 6
- rates: float32 [6], replicated, may hold values from 0 to 2, as said below
- step: int32 [1], replicated, may hold values from 1 to 3
Outputs:
- block_out: float32 [26112, 768], P(('dp', 'mp'))
- grad_norm: float32 [], replicated
- kernel_new: float32 [1024, 2304], P('mp')
- kernel_moments: float32 [2, 1024, 2304], P(None, 'mp')
- qkv_new: float32 [768, 2304], P('dp', 'mp')
- qkv_moments: float32 [2, 768, 2304], P(None, 'dp', 'mp')
- proj_new: float32 [768, 768], P('dp', 'mp')
- proj_moments: float32 [2, 768, 768], P(None, 'dp', 'mp')
- fc1_new: float32 [768, 3072], P('dp', 'mp')
- fc1_moments: float32 [2, 768, 3072], P(None, 'dp', 'mp')
- fc2_new: float32 [3072, 768], P('dp', 'mp')
- fc2_moments: float32 [2, 3072, 768], P(None, 'dp', 'mp')
- table_new: float32 [60, 768], replicated
- table_moments: float32 [2, 60, 768], replicated
Inputs may be any that keep to these rules, and one draw needn't show every extreme that they name: `kernel_state`: entry 2 of every state (the second moment) is positive. `qkv_state`: entry 2 is positive. `proj_state`: entry 2 is positive. `fc1_state`: entry 2 is positive. `fc2_state`: entry 2 is positive. `table_state`: entry 2 is positive. `rates`: Positive.
All inputs are finite; a program needn't handle non-finite values.
Results may differ from a plain program's by a relative error of at most 0.019.
Values may be sent and summed in bfloat16 or wider, within the bound.
No kernel may reach another device: no remote copies, remote signals or barrier semaphores. Data moves between devices by JAX's collectives and lax.ppermute only.
A program may use at most 256 MiB of HBM per device.

v0:
```python
import math

import jax
import jax.numpy as jnp
from jax import lax
from jax.sharding import PartitionSpec as P

D = 768
HEADS = 12
HEAD_DIM = 64
FF = 3072
BASE = 32
POS_GRID = 7
GRID_S = 28
GRID_L = 4
TROWS = 60


HIGHEST = lax.Precision.HIGHEST
NORM_EPS = 1e-06
BETA_ONE = 0.5
BETA_TWO = 0.5
DECAY = 0.05
ADAM_EPS = 1e-08
MASKED = -1e30


def to_low(array_in):
    return array_in.astype(jnp.bfloat16)


def matmul(left, right):
    return jnp.dot(left, right, preferred_element_type=jnp.float32)


def matmul_left(left, right):
    return lax.dot_general(
        left, right, (((0,), (0,)), ((), ())), preferred_element_type=jnp.float32
    )


def matmul_right(left, right):
    return lax.dot_general(
        left, right, (((1,), (1,)), ((), ())), preferred_element_type=jnp.float32
    )


def exact_left(left, right):
    return lax.dot_general(
        left, right, (((0,), (0,)), ((), ())), precision=HIGHEST, preferred_element_type=jnp.float32
    )


def norm_forward(inputs):
    centered = inputs - jnp.mean(inputs, axis=-1, keepdims=True)
    inverse = lax.rsqrt(jnp.mean(centered * centered, axis=-1, keepdims=True) + NORM_EPS)
    return (centered * inverse, inverse)


def norm_backward(upstream, normalized, inverse, gain_row):
    scaled = upstream * gain_row
    inner = jnp.mean(scaled * normalized, axis=-1, keepdims=True)
    result = inverse * (scaled - jnp.mean(scaled, axis=-1, keepdims=True) - normalized * inner)
    return (result, jnp.sum(upstream * normalized, axis=0), jnp.sum(upstream, axis=0))


def gelu_exact(inputs):
    return 0.5 * inputs * (1.0 + lax.erf(inputs * 0.7071067811865476))


def gelu_slope(inputs):
    return (
        0.5 * (1.0 + lax.erf(inputs * 0.7071067811865476))
        + inputs * jnp.exp(-0.5 * inputs * inputs) * 0.3989422804014327
    )


def image_ids(row_count):
    places = jnp.arange(row_count, dtype=jnp.int32)
    first_row = GRID_S * GRID_S
    return jnp.where(places < first_row, 0, 1 + (places - first_row) // (GRID_L * GRID_L))


def adam_step(state_stack, gradient, rate_value, factor, fix_one, fix_two):
    clipped = gradient * factor
    first_moment = BETA_ONE * state_stack[1] + (1.0 - BETA_ONE) * clipped
    second = BETA_TWO * state_stack[2] + (1.0 - BETA_TWO) * clipped * clipped
    movement = (
        first_moment / fix_one / (jnp.sqrt(second / fix_two) + ADAM_EPS) + DECAY * state_stack[0]
    )
    return (state_stack[0] - rate_value * movement, jnp.stack([first_moment, second]))


def body(
    kernel_state,
    qkv_state,
    proj_state,
    fc1_state,
    fc2_state,
    table_state,
    patches_s,
    patches_l,
    resize_s,
    resize_l,
    bilin_s,
    bilin_l,
    cotangent,
    rates,
    step,
):
    group_size = lax.axis_size("mp")
    qkv_low = to_low(qkv_state[0])
    proj_low = to_low(proj_state[0])
    fc1_low = to_low(fc1_state[0])
    fc2_low = to_low(fc2_state[0])
    by_rows = (
        lax.all_gather(qkv_low, "dp", axis=0, tiled=True),
        lax.all_gather(proj_low, "dp", axis=0, tiled=True),
        lax.all_gather(fc1_low, "dp", axis=0, tiled=True),
        lax.all_gather(fc2_low, "dp", axis=0, tiled=True),
    )
    w_qkv, w_proj, w_fc1, w_fc2 = (
        lax.all_gather(by_rows[0], "mp", axis=1, tiled=True),
        lax.all_gather(by_rows[1], "mp", axis=1, tiled=True),
        lax.all_gather(by_rows[2], "mp", axis=1, tiled=True),
        lax.all_gather(by_rows[3], "mp", axis=1, tiled=True),
    )
    base_rows = kernel_state[0]
    width = base_rows.shape[1] // 3
    small_flat = patches_s.reshape(-1, patches_s.shape[2])
    large_flat = patches_l.reshape(-1, patches_l.shape[2])
    small_tokens = patches_s.shape[1]
    large_tokens = patches_l.shape[0] * patches_l.shape[1] // group_size
    part_small = jnp.dot(resize_s, base_rows, precision=HIGHEST).reshape(-1, width)
    part_large = jnp.dot(resize_l, base_rows, precision=HIGHEST).reshape(-1, width)
    kern_small, kern_large = (
        lax.psum_scatter(part_small, "mp", scatter_dimension=1, tiled=True),
        lax.psum_scatter(part_large, "mp", scatter_dimension=1, tiled=True),
    )
    embed_small = matmul(small_flat, to_low(kern_small)).reshape(group_size, small_tokens, -1)
    embed_large = jnp.dot(large_flat.astype(jnp.float32), kern_large, precision=HIGHEST).reshape(
        group_size, large_tokens, -1
    )
    relaid = lax.all_to_all(
        jnp.concatenate([embed_small, embed_large], axis=1),
        "mp",
        split_axis=0,
        concat_axis=2,
        tiled=True,
    )
    embedded = relaid[0]
    table_rows = table_state[0]
    first_row = POS_GRID * POS_GRID
    grid_rows = table_rows[:first_row]
    pos_small = jnp.dot(bilin_s, grid_rows, precision=HIGHEST)
    pos_large = jnp.dot(bilin_l, grid_rows, precision=HIGHEST)
    images_large = large_tokens // bilin_l.shape[0]
    placed = (
        jnp.concatenate([pos_small, jnp.tile(pos_large, (images_large, 1))], axis=0)
        + table_rows[first_row]
    )
    inputs = embedded + placed
    row_count = inputs.shape[0]
    normal_one, inverse_one = norm_forward(inputs)
    normed_one = to_low(normal_one * table_rows[first_row + 1] + table_rows[first_row + 2])
    qkv_rows = to_low(matmul(normed_one, w_qkv))
    split_heads = qkv_rows.reshape(row_count, 3, HEADS, HEAD_DIM).transpose(1, 2, 0, 3)
    labels = image_ids(row_count)
    same_image = labels[:, None] == labels[None, :]
    scale = HEAD_DIM ** (-0.5)

    def head_scores(queries, key_rows):
        raw_scores = matmul_right(queries, key_rows) * scale
        return jnp.where(same_image, raw_scores, MASKED)

    def attend_head(pieces):
        scores = head_scores(pieces[0], pieces[1])
        largest = jnp.max(scores, axis=1, keepdims=True)
        exponent = jnp.exp(scores - largest)
        totals = jnp.sum(exponent, axis=1, keepdims=True)
        attended_head = matmul(to_low(exponent / totals), pieces[2])
        return (attended_head, (largest + jnp.log(totals))[:, 0])

    head_out, log_totals = lax.map(attend_head, (split_heads[0], split_heads[1], split_heads[2]))
    attended = to_low(head_out.transpose(1, 0, 2).reshape(row_count, -1))
    middle = inputs + matmul(attended, w_proj) + table_rows[first_row + 5]
    normal_two, inverse_two = norm_forward(middle)
    normed_two = to_low(normal_two * table_rows[first_row + 3] + table_rows[first_row + 4])
    hidden = matmul(normed_two, w_fc1) + table_rows[first_row + 7 :].reshape(-1)
    activated = to_low(gelu_exact(hidden))
    block_out = middle + matmul(activated, w_fc2) + table_rows[first_row + 6]
    upstream_low = to_low(cotangent)
    grad_fc2 = matmul_left(activated, upstream_low)
    bias_two_grad = jnp.sum(upstream_low.astype(jnp.float32), axis=0)
    hidden_grad = to_low(matmul_right(upstream_low, w_fc2) * gelu_slope(hidden))
    grad_fc1 = matmul_left(normed_two, hidden_grad)
    bias_one_grad = jnp.sum(hidden_grad.astype(jnp.float32), axis=0)
    norm_two_grad, gain_two_grad, shift_two_grad = norm_backward(
        matmul_right(hidden_grad, w_fc1), normal_two, inverse_two, table_rows[first_row + 3]
    )
    middle_grad = cotangent + norm_two_grad
    branch_low = to_low(middle_grad)
    grad_proj = matmul_left(attended, branch_low)
    bias_proj_grad = jnp.sum(branch_low.astype(jnp.float32), axis=0)
    attended_grad = (
        to_low(matmul_right(branch_low, w_proj))
        .reshape(row_count, HEADS, HEAD_DIM)
        .transpose(1, 0, 2)
    )

    def attend_back(pieces):
        queries, key_rows, value_rows, totals_log, out_grad = pieces
        probs = jnp.exp(head_scores(queries, key_rows) - totals_log[:, None])
        prob_grad = matmul_right(out_grad, value_rows)
        value_grad = matmul_left(to_low(probs), out_grad)
        score_grad = to_low(probs * (prob_grad - jnp.sum(probs * prob_grad, axis=1, keepdims=True)))
        return jnp.stack(
            [
                matmul(score_grad, key_rows) * scale,
                matmul_left(score_grad, queries) * scale,
                value_grad,
            ]
        )

    head_grads = lax.map(
        attend_back, (split_heads[0], split_heads[1], split_heads[2], log_totals, attended_grad)
    )
    qkv_grad = to_low(head_grads.transpose(2, 1, 0, 3).reshape(row_count, -1))
    grad_qkv = matmul_left(normed_one, qkv_grad)
    norm_one_grad, gain_one_grad, shift_one_grad = norm_backward(
        matmul_right(qkv_grad, w_qkv), normal_one, inverse_one, table_rows[first_row + 1]
    )
    input_grad = middle_grad + norm_one_grad
    large_grad = (
        input_grad[small_tokens:].reshape(images_large, -1, input_grad.shape[1]).sum(axis=0)
    )
    pos_grad = exact_left(bilin_s, input_grad[:small_tokens]) + exact_left(bilin_l, large_grad)
    vector_grads = jnp.stack(
        [
            jnp.sum(input_grad, axis=0),
            gain_one_grad,
            shift_one_grad,
            gain_two_grad,
            shift_two_grad,
            bias_proj_grad,
            bias_two_grad,
        ]
    )
    table_grad = jnp.concatenate(
        [pos_grad, vector_grads, bias_one_grad.reshape(-1, input_grad.shape[1])], axis=0
    )
    grad_low = to_low(input_grad)
    returned = lax.all_to_all(grad_low[None], "mp", split_axis=2, concat_axis=0, tiled=True)
    kern_small_grad = matmul_left(
        small_flat, returned[:, :small_tokens].reshape(-1, returned.shape[2])
    )
    kern_large_grad = matmul_left(
        large_flat, returned[:, small_tokens:].reshape(-1, returned.shape[2])
    )
    summed_small, summed_large = (
        lax.psum(kern_small_grad.astype(jnp.bfloat16), "dp").astype(jnp.float32),
        lax.psum(kern_large_grad.astype(jnp.bfloat16), "dp").astype(jnp.float32),
    )
    whole_small, whole_large = (
        lax.all_gather(summed_small.astype(jnp.bfloat16), "mp", axis=1, tiled=True).astype(
            summed_small.dtype
        ),
        lax.all_gather(summed_large.astype(jnp.bfloat16), "mp", axis=1, tiled=True).astype(
            summed_large.dtype
        ),
    )
    base_grad = exact_left(resize_s, whole_small.reshape(resize_s.shape[0], -1)) + exact_left(
        resize_l, whole_large.reshape(resize_l.shape[0], -1)
    )
    rows_summed = (
        lax.psum_scatter(
            grad_qkv.astype(jnp.bfloat16), "dp", scatter_dimension=0, tiled=True
        ).astype(jnp.float32),
        lax.psum_scatter(
            grad_proj.astype(jnp.bfloat16), "dp", scatter_dimension=0, tiled=True
        ).astype(jnp.float32),
        lax.psum_scatter(
            grad_fc1.astype(jnp.bfloat16), "dp", scatter_dimension=0, tiled=True
        ).astype(jnp.float32),
        lax.psum_scatter(
            grad_fc2.astype(jnp.bfloat16), "dp", scatter_dimension=0, tiled=True
        ).astype(jnp.float32),
    )
    owned_grads = (
        lax.psum_scatter(
            rows_summed[0].astype(jnp.bfloat16), "mp", scatter_dimension=1, tiled=True
        ).astype(jnp.float32),
        lax.psum_scatter(
            rows_summed[1].astype(jnp.bfloat16), "mp", scatter_dimension=1, tiled=True
        ).astype(jnp.float32),
        lax.psum_scatter(
            rows_summed[2].astype(jnp.bfloat16), "mp", scatter_dimension=1, tiled=True
        ).astype(jnp.float32),
        lax.psum_scatter(
            rows_summed[3].astype(jnp.bfloat16), "mp", scatter_dimension=1, tiled=True
        ).astype(jnp.float32),
    )
    squares = jnp.zeros((), jnp.float32)
    for owned_piece in owned_grads:
        squares = squares + jnp.sum(owned_piece * owned_piece)
    kernel_squares = jnp.where(lax.axis_index("dp") == 0, jnp.sum(base_grad * base_grad), 0.0)
    table_total, square_total = lax.psum((table_grad, squares + kernel_squares), ("dp", "mp"))
    grad_norm = jnp.sqrt(square_total + jnp.sum(table_total * table_total))
    clip_level = 0.5 * math.sqrt(3 * BASE * BASE * D + 4 * D * D + 2 * D * FF + TROWS * D)
    factor = clip_level / jnp.maximum(grad_norm, clip_level)
    step_count = step[0].astype(jnp.float32)
    fix_one = 1.0 - jnp.power(BETA_ONE, step_count)
    fix_two = 1.0 - jnp.power(BETA_TWO, step_count)
    kernel_new, kernel_moments = adam_step(
        kernel_state, base_grad, rates[0], factor, fix_one, fix_two
    )
    qkv_new, qkv_moments = adam_step(qkv_state, owned_grads[0], rates[1], factor, fix_one, fix_two)
    proj_new, proj_moments = adam_step(
        proj_state, owned_grads[1], rates[2], factor, fix_one, fix_two
    )
    fc1_new, fc1_moments = adam_step(fc1_state, owned_grads[2], rates[3], factor, fix_one, fix_two)
    fc2_new, fc2_moments = adam_step(fc2_state, owned_grads[3], rates[4], factor, fix_one, fix_two)
    table_new, table_moments = adam_step(
        table_state, table_total, rates[5], factor, fix_one, fix_two
    )
    return (
        block_out,
        grad_norm,
        kernel_new,
        kernel_moments,
        qkv_new,
        qkv_moments,
        proj_new,
        proj_moments,
        fc1_new,
        fc1_moments,
        fc2_new,
        fc2_moments,
        table_new,
        table_moments,
    )


def solution(mesh):
    placed = (
        P(None, "mp", None),
        P(None, "dp", "mp"),
        P(None, "dp", "mp"),
        P(None, "dp", "mp"),
        P(None, "dp", "mp"),
        P(),
        P("dp", None, None),
        P("dp", None, None),
        P(None, "mp"),
        P(None, "mp"),
        P(),
        P(),
        P(("dp", "mp"), None),
        P(),
        P(),
    )
    return jax.shard_map(
        body,
        mesh=mesh,
        in_specs=placed,
        out_specs=(
            P(("dp", "mp"), None),
            P(),
            P("mp", None),
            P(None, "mp", None),
            P("dp", "mp"),
            P(None, "dp", "mp"),
            P("dp", "mp"),
            P(None, "dp", "mp"),
            P("dp", "mp"),
            P(None, "dp", "mp"),
            P("dp", "mp"),
            P(None, "dp", "mp"),
            P(),
            P(),
        ),
        check_vma=False,
    )
```

profile of v0, /device:TPU:0, one launch (start us, length us, event | category | flops | bytes accessed | tf_op | source)
XLA Modules:
  0.0 1532.8 jit_solution(16620727584267823737)
XLA Ops:
  17.9 39.4 %fusion.56 = f32[2304,2304]{1,0:T(8,128)} fusion(f32[2304,512]{1,0:T(8,128)} %param.28, f32[3,512,2304]{2,1,0:T(8,128)} %param.19), kind=kOutput, calls=%fused_computation.76 | convolution fusion | flops 32614907904 | bytes 30670848 | tf_op jit(solution)/shard_map/dot_general | solution.py:135
  57.2 23.5 %reshape.328 = f32[6912,768]{1,0:T(8,128)} reshape(f32[2304,2304]{1,0:T(8,128)} %fusion.56) | data formatting | bytes 42467328 | tf_op jit(solution)/shard_map/reshape | solution.py:135
  84.0 26.9 %all_gather.32 = bf16[768,384]{1,0:T(8,128)(2,1)} all-gather(bf16[48,384]{1,0:T(8,128)(2,1)S(1)} %bitcast_convert_fusion.3), channel_id=1, replica_groups=mesh['dp'=16,'mp'=2] {'dp'}, dimensions={0}, use_global_device_ids=true | all-gather | bytes 626688 | tf_op jit(solution)/shard_map/all_gather | solution.py:118
  115.4 306.2 %reduce-scatter.19.cloned.1.call-done = f32[6912,384]{1,0:T(8,128)} async-done(((f32[6912,768]{1,0:T(8,128)}), f32[6912,384]{1,0:T(8,128)}) %reduce-scatter.19.cloned.1.call-update) | async-done | bytes 10616848 | tf_op jit(solution)/shard_map/reduce_scatter | solution.py:138
  451.6 11.5 all-to-all-done
  498.3 105.5 %while.24 = (s32[]{:T(128)}, bf16[12,816,64]{1,2,0:T(8,128)(2,1)}, f32[12,816]{1,0:T(8,128)}, bf16[12,816,64]{2,1,0:T(8,128)(2,1)S(1)}, bf16[12,816,64]{2,1,0:T(...) while((s32[]{:T(128)}, bf16[12,816,64]{1,2,0:T(8,128)(2,1)}, ...), condition=%wide.region_7.8_spmd.clone, body=%wide.region_4.7_spmd.clone.sunk | while | flops 180446160 | bytes 19823804 | solution.py:184
  609.5 10.9 multiply_convert_fusion.1
  620.5 11.6 convert_reduce_fusion
  648.7 119.9 %while.25 = (s32[]{:T(128)}, bf16[12,3,816,64]{2,3,1,0:T(8,128)(2,1)}, bf16[12,816,64]{2,1,0:T(8,128)(2,1)}, bf16[12,816,64]{2,1,0:T(8,128)(2,1)}, f32[12,816]{1...) while((s32[]{:T(128)}, ...), condition=%wide.region_14.15_spmd.clone, body=%wide.region_12.14_spmd.clone.sunk | while | flops 433954496 | bytes 22510944 | solution.py:225
  819.3 11.6 reduce.22
  835.4 19.9 %all_to_all.33 = bf16[2,2,156672]{2,1,0:T(2,128)(2,1)} all-to-all(bf16[2,2,156672]{2,1,0:T(2,128)(2,1)} %reshape.357), channel_id=1, replica_groups=mesh['dp'=16,'mp'=2] {'mp'}, dimensions={0} | all-to-all | bytes 2506752 | tf_op jit(solution)/shard_map/all_to_all | solution.py:253
  876.6 48.7 %reduce-scatter.29.cloned.1.call-done = bf16[192,768]{1,0:T(8,128)(2,1)} async-done(((bf16[3072,768]{1,0:T(8,128)(2,1)}), bf16[192,768]{1,0:T(8,128)(2,1)}) %reduce-scatter.29.cloned.1.call-update) | async-done | bytes 294928 | tf_op jit(solution)/shard_map/reduce_scatter | solution.py:285
  927.3 77.6 %reduce-scatter.25.cloned.1.call-done = bf16[48,3072]{1,0:T(8,128)(2,1)} async-done(((bf16[768,3072]{1,0:T(8,128)(2,1)}), bf16[48,3072]{1,0:T(8,128)(2,1)}) %reduce-scatter.25.cloned.1.call-update) | async-done | bytes 294928 | tf_op jit(solution)/shard_map/reduce_scatter | solution.py:282
  1005.0 131.2 %all-reduce.6.cloned.1.call-done = (bf16[6912,384]{0,1:T(8,128)(2,1)}, bf16[192,384]{1,0:T(8,128)(2,1)}) async-done(((bf16[6912,384]{0,1:T(8,128)(2,1)}, bf16[192,384]{1,0:T(8,128)(2,1)}), (bf16[6912,384]{0,1:T(8,128)(2,1)}, bf16[192,384]{1,0:T(8,128)(2,1)})) %all-reduce.6.cloned.1.call-update) | async-done | bytes 5455888 | tf_op jit(solution)/shard_map/psum | solution.py:262
  1136.9 13.0 fusion.145
  1192.5 10.4 all_gather.38
  1203.0 74.2 %reduce-scatter.31.cloned.1.call-done = bf16[1152,48]{1,0:T(8,128)(2,1)} async-done(((bf16[2304,48]{1,0:T(8,128)(2,1)}), bf16[1152,48]{1,0:T(8,128)(2,1)}) %reduce-scatter.31.cloned.1.call-update) | async-done | bytes 110608
  1280.3 12.7 reduce-scatter.35.cloned.1.call-done
  1294.8 12.5 reduce-scatter.27.cloned.1.call-done
  1310.2 14.5 copy.103
  1324.7 16.5 %reshape.335 = bf16[2304,2304]{1,0:T(8,128)(2,1)} reshape(bf16[6912,768]{1,0:T(8,128)(2,1)} %copy.103) | data formatting | bytes 21233664 | tf_op jit(solution)/shard_map/reshape | solution.py:273
  1341.3 20.9 %fusion.149 = f32[2304,512]{1,0:T(8,128)S(1)} fusion(bf16[2304,2304]{1,0:T(8,128)(2,1)} %reshape.335, f32[2304,512]{1,0:T(8,128)} %param.28), kind=kOutput, calls=%fused_computation.249 | convolution fusion | flops 32614907904 | bytes 20054016 | tf_op jit(solution)/shard_map/dot_general | solution.py:49
  1368.1 69.1 %all-reduce.4.cloned.1.call-done = f32[60,768]{1,0:T(8,128)} async-done(((f32[60,768]{1,0:T(8,128)}), f32[60,768]{1,0:T(8,128)}) %all-reduce.4.cloned.1.call-update) | async-done | bytes 184336 | tf_op jit(solution)/shard_map/psum | solution.py:307
  1438.8 41.3 %psum.30 = f32[]{:T(128)} all-reduce(f32[]{:T(128)S(6)} %add.360), channel_id=1, replica_groups=mesh['dp'=16,'mp'=2] {'dp','mp'}, use_global_device_ids=true, to_apply=%region_32.33 | all-reduce | flops 1 | bytes 8 | tf_op jit(solution)/shard_map/psum | solution.py:307
  (435 shorter events, 504.2 us)
Async XLA Ops:
  8.0 413.6 %copy-start = (bf16[4,16,6912]{2,1,0:T(8,128)(2,1)S(1)}, bf16[4,16,6912]{2,1,0:T(8,128)(2,1)}, u32[]{:S(2)}) copy-start(bf16[4,16,6912]{2,1,0:T(8,128)(2,1)} %param.26) | copy-start | bytes 2654212
  8.0 74.6 %all-gather.9.cloned.1.call-start = ((), (), s32[]{:S(2)}) async-start(), calls=%async_computation.14 | async-start | bytes 1880064 | tf_op jit(solution)/shard_map/all_gather | solution.py:117
  9.8 101.2 %all-gather.15.cloned.1.call-start = ((), (), s32[]{:S(2)}) async-start(), calls=%async_computation.17 | async-start | bytes 2506752 | tf_op jit(solution)/shard_map/all_gather | solution.py:119
  11.5 102.1 %reduce-scatter.17.cloned.1.call-start = ((), (), s32[]{:S(2)}) async-start(), calls=%async_computation.12 | async-start | bytes 884736 | tf_op jit(solution)/shard_map/reduce_scatter | solution.py:137
  17.8 403.8 %reduce-scatter.19.cloned.1.call-start = ((), (), s32[]{:S(2)}) async-start(), calls=%async_computation.13 | async-start | bytes 31850496 | tf_op jit(solution)/shard_map/reduce_scatter | solution.py:138
  80.8 370.7 %all-gather.19.cloned.1.call-start = ((), (), s32[]{:S(2)}) async-start(), calls=%async_computation.19 | async-start | bytes 2506752 | tf_op jit(solution)/shard_map/all_gather | solution.py:120
  82.5 386.7 %all-gather.11.cloned.1.call-start = ((), (), s32[]{:S(2)}) async-start(), calls=%async_computation.15 | async-start | bytes 5308416 | tf_op jit(solution)/shard_map/all_gather | solution.py:123
  83.1 520.7 %all-gather.13.cloned.1.call-start = ((), (), s32[]{:S(2)}) async-start(), calls=%async_computation.16 | async-start | bytes 1769472 | tf_op jit(solution)/shard_map/all_gather | solution.py:124
  110.9 498.6 %all-gather.17.cloned.1.call-start = ((), (), s32[]{:S(2)}) async-start(), calls=%async_computation.18 | async-start | bytes 7077888 | tf_op jit(solution)/shard_map/all_gather | solution.py:125
  429.9 33.2 %all-to-all-start = ((f32[2,816,384]{2,1,0:T(8,128)}), f32[2,816,384]{2,1,0:T(8,128)S(1)}, u32[]{:S(2)}, u32[]{:S(2)}) async-start(f32[2,816,384]{2,1,0:T(8,128)} %pad_maximum_fusion.1), calls=%async_computation.2 | async-start | bytes 5013504 | tf_op jit(solution)/shard_map/all_to_all | solution.py:144
  433.7 186.8 %all-gather.21.cloned.1.call-start = ((), (), s32[]{:S(2)}) async-start(), calls=%async_computation.20 | async-start | bytes 7077888 | tf_op jit(solution)/shard_map/all_gather | solution.py:126
  451.5 421.2 %reduce-scatter.23.cloned.1.call-start = ((), (), s32[]{:S(2)}) async-start(), calls=%async_computation.22 | async-start | bytes 1253376 | tf_op jit(solution)/shard_map/reduce_scatter | solution.py:279
  609.0 179.3 %copy-start.6 = (f32[816,768]{1,0:T(8,128)}, f32[816,768]{1,0:T(8,128)S(1)}, u32[]{:S(2)}) copy-start(f32[816,768]{1,0:T(8,128)S(1)} %get-tuple-element.323) | copy-start | bytes 7520260
  648.6 225.9 %reduce-scatter.21.cloned.1.call-start = ((), (), s32[]{:S(2)}) async-start(), calls=%async_computation.21 | async-start | bytes 3760128 | tf_op jit(solution)/shard_map/reduce_scatter | solution.py:276
  779.0 146.4 %reduce-scatter.29.cloned.1.call-start = ((), (), s32[]{:S(2)}) async-start(), calls=%async_computation.25 | async-start | bytes 5013504 | tf_op jit(solution)/shard_map/reduce_scatter | solution.py:285
  788.3 216.6 %reduce-scatter.25.cloned.1.call-start = ((), (), s32[]{:S(2)}) async-start(), calls=%async_computation.23 | async-start | bytes 5013504 | tf_op jit(solution)/shard_map/reduce_scatter | solution.py:282
  798.3 337.9 %all-reduce.6.cloned.1.call-start = ((), (), s32[]{:S(2)}) async-start(), calls=%async_computation.31 | async-start | bytes 10911744 | tf_op jit(solution)/shard_map/psum | solution.py:262
  872.7 318.2 %reduce-scatter.33.cloned.1.call-start = ((), (), s32[]{:S(2)}) async-start(), calls=%async_computation.29 | async-start | bytes 294912
  874.5 402.8 %reduce-scatter.31.cloned.1.call-start = ((), (), s32[]{:S(2)}) async-start(), calls=%async_computation.28 | async-start | bytes 884736
  876.6 416.5 %reduce-scatter.35.cloned.1.call-start = ((), (), s32[]{:S(2)}) async-start(), calls=%async_computation.30 | async-start | bytes 589824
  927.2 380.1 %reduce-scatter.27.cloned.1.call-start = ((), (), s32[]{:S(2)}) async-start(), calls=%async_computation.24 | async-start | bytes 442368 | tf_op jit(solution)/shard_map/reduce_scatter | solution.py:296
  1004.9 305.3 %all-gather.23.cloned.1.call-start = ((), (), s32[]{:S(2)}) async-start(), calls=%async_computation.26 | async-start | bytes 15925248 | tf_op jit(solution)/shard_map/all_gather | solution.py:268
  1136.2 301.0 %all-reduce.4.cloned.1.call-start = ((), (), s32[]{:S(2)}) async-start(), calls=%async_computation.27 | async-start | bytes 393216 | tf_op jit(solution)/shard_map/psum | solution.py:307
  1362.2 119.3 %copy-start.15 = (f32[3,60,768]{2,1,0:T(8,128)S(1)}, f32[3,60,768]{2,1,0:T(8,128)}, u32[]{:S(2)}) copy-start(f32[3,60,768]{2,1,0:T(8,128)} %param.24) | copy-start | bytes 1658884
  (45 other events, 457.7 us)
Sparse Core Ops, SparseCore 0:
  11.6 43.0 all-gather.8
  57.5 41.2 all-gather.14
  101.7 40.7 all-gather.18
  143.9 71.4 all-gather.10
  216.7 46.7 all-gather.12
  264.9 84.6 all-gather.16
  451.6 64.0 all-gather.20
  648.8 57.9 reduce-scatter.22
  779.1 68.0 reduce-scatter.20
  850.9 74.4 reduce-scatter.28
  930.3 74.5 reduce-scatter.24
  1009.1 127.0 all-reduce.5
  1139.1 10.7 reduce-scatter.32
  1152.7 124.4 reduce-scatter.30
  1279.9 13.1 reduce-scatter.34
  1295.2 12.0 reduce-scatter.26
  1314.2 122.9 all-reduce.3
Sparse Core Ops, SparseCore 1:
  17.9 17.9 reduce-scatter.16
  80.8 340.7 reduce-scatter.18
  1136.3 134.1 all-gather.22
where the time goes:
time: 1550 us; the launch traced here: 1530 us
  waiting for transfers between devices  745 us (48%)
  matrix products  339 us (22%)
  local copies, waits for them, and re-layouts  245 us (16%)
  blocking collectives  98.5 us (6%)
  other arithmetic  76.2 us (5%)
  between operations  23.3 us (2%)
    reduce_scatter x1, waiting for transfers between devices, body(): lax.psum_scatter(part_large, 'mp', scatter_dimension=1, tiled=True)  306 us
    psum x1, waiting for transfers between devices, body(): lax.psum(kern_large_grad.astype(jnp.bfloat16), 'dp').astype(jnp.float32)  131 us
    dot_general x29, matrix products, matmul(): return jnp.dot(left, right, preferred_element_type=jnp.float32)  92.4 us
    dot_general x40, matrix products, matmul_right(): lax.dot_general(left, right, (((1,), (1,)), ((), ())), preferred_element_...  89.6 us
    unnamed x23, waiting for transfers between devices  88.2 us
    reduce_scatter x1, waiting for transfers between devices, body(): lax.psum_scatter(grad_fc1.astype(jnp.bfloat16), 'dp', scatter_dimension=0...  77.6 us
    unnamed x94, local copies, waits for them, and re-layouts  75 us
    dot_general x30, matrix products, matmul_left(): lax.dot_general(left, right, (((0,), (0,)), ((), ())), preferred_element_...  69.4 us
  transfers between devices with their start and end apart: 21, of which 9 were waited for; matrix products, arithmetic and copies ran while one was open for 37% of the time, Pallas kernels for 0%

commit v1 on v0

v1 whole, which is shorter than its diff:
```python
import functools
import math

import jax
import jax.numpy as jnp
from jax import lax
from jax.experimental import pallas as pl
from jax.experimental.pallas import tpu as pltpu
from jax.sharding import PartitionSpec as P

D = 768
HEADS = 12
HEAD_DIM = 64
FF = 3072
BASE = 32
POS_GRID = 7
GRID_S = 28
GRID_L = 4
TROWS = 60

NORM_EPS = 1e-06
BETA_ONE = 0.5
BETA_TWO = 0.5
DECAY = 0.05
ADAM_EPS = 1e-08
MASKED = -1e30
LOG2E = 1.4426950408889634
LANES = 128
MIB = 2**20

BF = jnp.bfloat16
F32 = jnp.float32
NN = (((1,), (0,)), ((), ()))
NT = (((1,), (1,)), ((), ()))
TN = (((0,), (0,)), ((), ()))


def shape_of(dims, dtype):
    return jax.ShapeDtypeStruct(dims, dtype)


def params(mib=56):
    return pltpu.CompilerParams(vmem_limit_bytes=mib * MIB)


def cost(flops, moved):
    return pl.CostEstimate(flops=int(flops), bytes_accessed=int(moved), transcendentals=0)


def dot(left, right, dims=NN):
    return lax.dot_general(left, right, dims, preferred_element_type=F32)


def halves(value):
    high = value.astype(BF)
    return high, (value - high.astype(F32)).astype(BF)


def dot_fine(left, right, dims=NN):
    left_high, left_low = halves(left)
    right_high, right_low = halves(right)
    return dot(left_high, right_high, dims) + (
        dot(left_high, right_low, dims) + dot(left_low, right_high, dims)
    )


def norm_forward(inputs):
    centered = inputs - jnp.mean(inputs, axis=-1, keepdims=True)
    inverse = lax.rsqrt(jnp.mean(centered * centered, axis=-1, keepdims=True) + NORM_EPS)
    return centered * inverse, inverse


def norm_backward(upstream, normalized, inverse, gain_row):
    scaled = upstream * gain_row
    inner = jnp.mean(scaled * normalized, axis=-1, keepdims=True)
    result = inverse * (scaled - jnp.mean(scaled, axis=-1, keepdims=True) - normalized * inner)
    return (
        result,
        jnp.sum(upstream * normalized, axis=0, keepdims=True),
        jnp.sum(upstream, axis=0, keepdims=True),
    )


def resize_kernel(
    base_ref, small_ref, large_ref, patch_ref, projected_ref, embed_ref, kern_ref, turned, pixels_ref
):
    rows = embed_ref.shape[0]

    @pl.when(pl.program_id(0) == 0)
    def _():
        embed_ref[...] = jnp.zeros_like(embed_ref)
        kern_ref[...] = jnp.zeros_like(kern_ref)
        count = large_ref.shape[0]
        for start in range(0, rows, LANES):
            size = min(LANES, rows - start)
            patch = patch_ref[start : start + size, :].astype(F32)
            if size < LANES:
                patch = jnp.concatenate(
                    [patch, jnp.zeros((LANES - size, patch.shape[1]), F32)], axis=0
                )
            turned[...] = patch.T
            for channel in range(3):
                pixels_ref[:, channel * rows + start : channel * rows + start + size] = turned[
                    pl.ds(channel, count, stride=3), :
                ][:, :size].astype(BF)

    base = base_ref[0]
    width = base.shape[1] // 3
    large_high, large_low = halves(large_ref[...])
    pixels = pixels_ref[...]
    projected = dot(large_high, pixels, TN) + dot(large_low, pixels, TN)
    projected_ref[...] = projected.astype(BF)
    kern_ref[...] += dot_fine(small_ref[...], base)
    total = embed_ref[...]
    for channel in range(3):
        total += dot_fine(
            projected[:, channel * rows : (channel + 1) * rows],
            base[:, channel * width : (channel + 1) * width],
            TN,
        )
    embed_ref[...] = total


def resize_forward(kernel_state, resize_s, resize_l, patches):
    base_rows, wide = kernel_state.shape[1:]
    count = base_rows // LANES
    rows = patches.shape[0]
    columns = 3 * rows
    return pl.pallas_call(
        resize_kernel,
        grid=(count,),
        in_specs=[
            pl.BlockSpec((1, LANES, wide), lambda i: (0, i, 0)),
            pl.BlockSpec((resize_s.shape[0], LANES), lambda i: (0, i)),
            pl.BlockSpec((resize_l.shape[0], LANES), lambda i: (0, i)),
            pl.BlockSpec(patches.shape, lambda i: (0, 0)),
        ],
        out_specs=[
            pl.BlockSpec((LANES, columns), lambda i: (i, 0)),
            pl.BlockSpec((rows, wide // 3), lambda i: (0, 0)),
            pl.BlockSpec((resize_s.shape[0], wide), lambda i: (0, 0)),
        ],
        out_shape=[
            shape_of((base_rows, columns), BF),
            shape_of((rows, wide // 3), F32),
            shape_of((resize_s.shape[0], wide), F32),
        ],
        scratch_shapes=[
            pltpu.VMEM((patches.shape[1], LANES), F32),
            pltpu.VMEM((resize_l.shape[0], columns), BF),
        ],
        compiler_params=params(),
        cost_estimate=cost(9e9, 0),
        name="resize",
    )(kernel_state, resize_s, resize_l, patches)


def embed_kernel(
    patch_ref, kern_ref, large_ref, bilin_s_ref, bilin_l_ref, table_ref, x_ref, a_ref, woven
):
    table = table_ref[0]
    first = POS_GRID * POS_GRID
    pixels = kern_ref.shape[0]
    width = table.shape[1]
    tiles = width // LANES
    for channel in range(3):
        for tile in range(tiles):
            start = channel * width + tile * LANES
            woven[tile, pl.ds(channel, pixels, stride=3), :] = kern_ref[:, start : start + LANES]
    kern = jnp.concatenate([woven[tile].astype(BF) for tile in range(tiles)], axis=1)
    grid_rows = table[:first]
    bias = table[first : first + 1]
    small = patch_ref.shape[0]
    x_ref[:small, :] = (
        dot(patch_ref[...], kern) + dot_fine(bilin_s_ref[...], grid_rows) + bias
    )
    tokens = bilin_l_ref.shape[0]
    placed = dot_fine(bilin_l_ref[...], grid_rows) + bias
    for image in range(large_ref.shape[0] // tokens):
        part = slice(image * tokens, (image + 1) * tokens)
        x_ref[small + image * tokens : small + (image + 1) * tokens, :] = large_ref[part, :] + placed
    normal, _ = norm_forward(x_ref[...])
    a_ref[...] = (normal * table[first + 1 : first + 2] + table[first + 2 : first + 3]).astype(BF)


def embed(patches, kern, large, bilin_s, bilin_l, table_state):
    rows = patches.shape[0] + large.shape[0]
    width = table_state.shape[2]
    whole = lambda array: pl.BlockSpec(array.shape, lambda i: (0,) * array.ndim)
    return pl.pallas_call(
        embed_kernel,
        grid=(1,),
        in_specs=[
            whole(patches),
            whole(kern),
            whole(large),
            whole(bilin_s),
            whole(bilin_l),
            pl.BlockSpec((1,) + table_state.shape[1:], lambda i: (0, 0, 0)),
        ],
        out_specs=[pl.BlockSpec((rows, width), lambda i: (0, 0))] * 2,
        out_shape=[shape_of((rows, width), F32), shape_of((rows, width), BF)],
        scratch_shapes=[pltpu.VMEM((width // LANES, patches.shape[1], LANES), F32)],
        compiler_params=params(),
        cost_estimate=cost(5e9, 0),
        name="embed",
    )(patches, kern, large, bilin_s, bilin_l, table_state)


def product_kernel(left_ref, right_ref, out_ref):
    out_ref[...] = dot(left_ref[...], right_ref[...]).astype(BF)


def product(left, right, block):
    rows, depth = left.shape
    columns = right.shape[1]
    return pl.pallas_call(
        product_kernel,
        grid=(columns // block,),
        in_specs=[
            pl.BlockSpec((rows, depth), lambda i: (0, 0)),
            pl.BlockSpec((depth, block), lambda i: (0, i)),
        ],
        out_specs=pl.BlockSpec((rows, block), lambda i: (0, i)),
        out_shape=shape_of((rows, columns), BF),
        compiler_params=params(),
        cost_estimate=cost(7e9, 0),
        name="project",
    )(left, right)


def image_features(rows, first_rows, image_rows):
    row = lax.broadcasted_iota(jnp.int32, (rows, LANES), 0)
    lane = lax.broadcasted_iota(jnp.int32, (rows, LANES), 1) % HEAD_DIM
    label = jnp.where(row < first_rows, 0, 1 + (row - first_rows) // image_rows)
    count = 1 + (rows - first_rows) // image_rows
    own = label == lane
    query = jnp.where(own | (lane >= count), 0.0, MASKED).astype(BF)
    return query, jnp.where(own, 1.0, 0.0).astype(BF)


def attend_kernel(first_rows, image_rows, chunks, q_ref, k_ref, v_ref, out_ref, log_ref):
    rows = q_ref.shape[0]
    query_mark, key_mark = image_features(rows, first_rows, image_rows)
    low = lax.broadcasted_iota(jnp.int32, (rows, LANES), 1) < HEAD_DIM
    step = rows // chunks
    queries = q_ref[...] * jnp.asarray(HEAD_DIM**-0.5, BF)
    keys, values = k_ref[...], v_ref[...]
    ones = jnp.ones((rows, LANES), BF)
    results = []
    for head in range(2):
        mine = low if head == 0 else ~low
        query = jnp.where(mine, queries, query_mark)
        key = jnp.where(mine, keys, key_mark)
        value = jnp.where(mine, values, ones)
        outs, logs = [], []
        for chunk in range(chunks):
            scores = dot(query[chunk * step : (chunk + 1) * step], key, NT)
            largest = jnp.max(scores, axis=1, keepdims=True)
            probs = jnp.exp2(scores * LOG2E - largest * LOG2E)
            summed = dot(probs.astype(BF), value)
            rolled = pltpu.roll(summed, HEAD_DIM, 1)
            outs.append(summed / rolled)
            logs.append(largest * LOG2E + jnp.log2(jnp.where(mine[:step], rolled, summed)))
        results.append(jnp.concatenate(outs, axis=0))
        log_ref[0, 8 * head : 8 * head + 8, :] = jnp.concatenate(logs, axis=0).T[:8]
    out_ref[...] = jnp.where(low, results[0], results[1]).astype(BF)


def attend(qkv, first_rows, image_rows):
    rows, wide = qkv.shape
    width = wide // 3
    pairs = width // LANES
    chunks = 3 if rows % 48 == 0 else 1
    part = lambda offset: pl.BlockSpec((rows, LANES), lambda i: (0, offset + i))
    return pl.pallas_call(
        functools.partial(attend_kernel, first_rows, image_rows, chunks),
        grid=(pairs,),
        in_specs=[part(0), part(pairs), part(2 * pairs)],
        out_specs=[part(0), pl.BlockSpec((1, 16, rows), lambda i: (i, 0, 0))],
        out_shape=[shape_of((rows, width), BF), shape_of((pairs, 16, rows), F32)],
        compiler_params=params(),
        cost_estimate=cost(18e9, 0),
        name="attend",
    )(qkv, qkv, qkv)


def merge_kernel(x_ref, attended_ref, w_ref, table_ref, middle_ref, a_ref):
    first = POS_GRID * POS_GRID
    table = table_ref[0]
    middle = x_ref[...] + dot(attended_ref[...], w_ref[...]) + table[first + 5 : first + 6]
    middle_ref[...] = middle
    normal, _ = norm_forward(middle)
    a_ref[...] = (normal * table[first + 3 : first + 4] + table[first + 4 : first + 5]).astype(BF)


def merge(inputs, attended, w_proj, table_state):
    rows, width = inputs.shape
    whole = lambda array: pl.BlockSpec(array.shape, lambda i: (0,) * array.ndim)
    return pl.pallas_call(
        merge_kernel,
        grid=(1,),
        in_specs=[
            whole(inputs),
            whole(attended),
            whole(w_proj),
            pl.BlockSpec((1,) + table_state.shape[1:], lambda i: (0, 0, 0)),
        ],
        out_specs=[whole(inputs)] * 2,
        out_shape=[shape_of((rows, width), F32), shape_of((rows, width), BF)],
        compiler_params=params(),
        cost_estimate=cost(6e9, 0),
        name="merge",
    )(inputs, attended, w_proj, table_state)


def feed_kernel(
    middle_ref,
    a_ref,
    cotangent_ref,
    w_one_ref,
    w_two_ref,
    bias_ref,
    table_ref,
    out_ref,
    grad_ref,
    g_one_ref,
    g_two_ref,
    b_one_ref,
    b_two_ref,
    turned,
    upstream,
):
    @pl.when(pl.program_id(0) == 0)
    def _():
        first = POS_GRID * POS_GRID
        turned[...] = a_ref[...].T
        low = cotangent_ref[...].astype(BF)
        upstream[...] = low
        out_ref[...] = middle_ref[...] + table_ref[0][first + 6 : first + 7]
        grad_ref[...] = jnp.zeros_like(grad_ref)
        b_two_ref[...] = jnp.sum(low.astype(F32), axis=0, keepdims=True)

    w_one, w_two, dz = w_one_ref[...], w_two_ref[...], upstream[...]
    hidden = dot(a_ref[...], w_one) + bias_ref[...]
    phi = 0.5 * (1.0 + lax.erf(hidden * 0.7071067811865476))
    active = (hidden * phi).astype(BF)
    slope = phi + hidden * jnp.exp(-0.5 * hidden * hidden) * 0.3989422804014327
    change = dot(dz, w_two, NT) * slope
    b_one_ref[...] = jnp.sum(change, axis=0, keepdims=True)
    change = change.astype(BF)
    out_ref[...] += dot(active, w_two)
    grad_ref[...] += dot(change, w_one, NT)
    g_one_ref[...] = dot(turned[...], change).astype(BF)
    g_two_ref[...] = dot(active, dz, TN).astype(BF)


def feed(middle, normed, cotangent, w_one, w_two, bias_one, table_state, block):
    rows, width = normed.shape
    hidden = w_one.shape[1]
    full = pl.BlockSpec((rows, width), lambda i: (0, 0))
    across = pl.BlockSpec((width, block), lambda i: (0, i))
    down = pl.BlockSpec((block, width), lambda i: (i, 0))
    line = pl.BlockSpec((1, block), lambda i: (0, i))
    return pl.pallas_call(
        feed_kernel,
        grid=(hidden // block,),
        in_specs=[
            full,
            full,
            full,
            across,
            down,
            line,
            pl.BlockSpec((1,) + table_state.shape[1:], lambda i: (0, 0, 0)),
        ],
        out_specs=[full, full, across, down, line, pl.BlockSpec((1, width), lambda i: (0, 0))],
        out_shape=[
            shape_of((rows, width), F32),
            shape_of((rows, width), F32),
            shape_of((width, hidden), BF),
            shape_of((hidden, width), BF),
            shape_of((1, hidden), F32),
            shape_of((1, width), F32),
        ],
        scratch_shapes=[pltpu.VMEM((width, rows), BF), pltpu.VMEM((rows, width), BF)],
        compiler_params=params(60),
        cost_estimate=cost(34e9, 0),
        name="feed",
    )(middle, normed, cotangent, w_one, w_two, bias_one, table_state)


def merge_back_kernel(
    grad_ref,
    middle_ref,
    cotangent_ref,
    attended_ref,
    w_ref,
    table_ref,
    back_ref,
    heads_ref,
    g_ref,
    rows_ref,
):
    first = POS_GRID * POS_GRID
    normal, inverse = norm_forward(middle_ref[...])
    change, gain, shift = norm_backward(
        grad_ref[...], normal, inverse, table_ref[0][first + 3 : first + 4]
    )
    back = cotangent_ref[...] + change
    back_ref[...] = back
    low = back.astype(BF)
    heads_ref[...] = dot(low, w_ref[...], NT).astype(BF)
    g_ref[...] = dot(attended_ref[...], low, TN).astype(BF)
    rows_ref[0:1, :] = gain
    rows_ref[1:2, :] = shift
    rows_ref[2:3, :] = jnp.sum(low.astype(F32), axis=0, keepdims=True)


def merge_back(grad, middle, cotangent, attended, w_proj, table_state):
    rows, width = middle.shape
    whole = lambda array: pl.BlockSpec(array.shape, lambda i: (0,) * array.ndim)
    return pl.pallas_call(
        merge_back_kernel,
        grid=(1,),
        in_specs=[
            whole(grad),
            whole(middle),
            whole(cotangent),
            whole(attended),
            whole(w_proj),
            pl.BlockSpec((1,) + table_state.shape[1:], lambda i: (0, 0, 0)),
        ],
        out_specs=[
            whole(middle),
            whole(middle),
            whole(w_proj),
            pl.BlockSpec((8, width), lambda i: (0, 0)),
        ],
        out_shape=[
            shape_of((rows, width), F32),
            shape_of((rows, width), BF),
            shape_of(w_proj.shape, BF),
            shape_of((8, width), F32),
        ],
        compiler_params=params(),
        cost_estimate=cost(9e9, 0),
        name="merge_back",
    )(grad, middle, cotangent, attended, w_proj, table_state)


def attend_back_kernel(
    first_rows, image_rows, chunks, q_ref, k_ref, v_ref, out_ref, up_ref, log_ref, grad_ref
):
    rows = q_ref.shape[0]
    query_mark, key_mark = image_features(rows, first_rows, image_rows)
    low = lax.broadcasted_iota(jnp.int32, (rows, LANES), 1) < HEAD_DIM
    step = rows // chunks
    queries = q_ref[...] * jnp.asarray(HEAD_DIM**-0.5, BF)
    keys, values, up = k_ref[...], v_ref[...], up_ref[...]
    overlap = (out_ref[...].astype(F32) * up.astype(F32)).T
    zeros = jnp.zeros((rows, LANES), BF)
    grads = ([], [], [])
    for head in range(2):
        mine = low if head == 0 else ~low
        query = jnp.where(mine, queries, query_mark)
        key = jnp.where(mine, keys, key_mark)
        value = jnp.where(mine, values, zeros)
        inner = jnp.sum(overlap[HEAD_DIM * head : HEAD_DIM * (head + 1)], axis=0, keepdims=True)
        totals = log_ref[0, 8 * head : 8 * head + 1, :]
        query_grad = jnp.zeros((rows, LANES), F32)
        key_grads, value_grads = [], []
        for chunk in range(chunks):
            part = slice(chunk * step, (chunk + 1) * step)
            scores = dot(key[part], query, NT)
            probs = jnp.exp2(scores * LOG2E - totals)
            value_grads.append(dot(probs.astype(BF), up))
            change = (probs * (dot(value[part], up, NT) - inner)).astype(BF)
            key_grads.append(dot(change, queries))
            query_grad = query_grad + dot(change, keys[part], TN)
        grads[0].append(query_grad * HEAD_DIM**-0.5)
        grads[1].append(jnp.concatenate(key_grads, axis=0))
        grads[2].append(jnp.concatenate(value_grads, axis=0))
    for place, pair in enumerate(grads):
        grad_ref[place] = jnp.where(low, pair[0], pair[1]).astype(BF)


def attend_back(qkv, attended, upstream, logs, first_rows, image_rows):
    rows, wide = qkv.shape
    width = wide // 3
    pairs = width // LANES
    part = lambda offset: pl.BlockSpec((rows, LANES), lambda i: (0, offset + i))
    return pl.pallas_call(
        functools.partial(attend_back_kernel, first_rows, image_rows, 1),
        grid=(pairs,),
        in_specs=[
            part(0),
            part(pairs),
            part(2 * pairs),
            part(0),
            part(0),
            pl.BlockSpec((1, 16, rows), lambda i: (i, 0, 0)),
        ],
        out_specs=pl.BlockSpec((3, rows, LANES), lambda i: (0, 0, i)),
        out_shape=shape_of((3, rows, width), BF),
        compiler_params=params(),
        cost_estimate=cost(30e9, 0),
        name="attend_back",
    )(qkv, qkv, qkv, attended, upstream, logs)


def inputs_back_kernel(
    heads_ref,
    a_ref,
    w_ref,
    x_ref,
    back_ref,
    table_ref,
    patch_ref,
    bilin_s_ref,
    bilin_l_ref,
    middle_rows_ref,
    b_one_ref,
    b_two_ref,
    g_ref,
    table_grad_ref,
    large_ref,
    kern_ref,
    turned,
    total,
    woven,
):
    place = pl.program_id(0)

    @pl.when(place == 0)
    def _():
        turned[...] = a_ref[...].T
        total[...] = jnp.zeros_like(total)

    heads = heads_ref[0]
    g_ref[...] = dot(turned[...], heads).astype(BF)
    total[...] += dot(heads, w_ref[...], NT)

    @pl.when(place == pl.num_programs(0) - 1)
    def _():
        first = POS_GRID * POS_GRID
        normal, inverse = norm_forward(x_ref[...])
        change, gain, shift = norm_backward(
            total[...], normal, inverse, table_ref[0][first + 1 : first + 2]
        )
        grad = back_ref[...] + change
        low = grad.astype(BF)
        small = patch_ref.shape[0]
        width = grad.shape[1]
        large_ref[...] = low[small:]
        kern = dot(patch_ref[...], low[:small], TN)
        pixels = kern_ref.shape[0]
        for tile in range(width // LANES):
            woven[tile] = kern[:, tile * LANES : (tile + 1) * LANES]
            for channel in range(3):
                start = channel * width + tile * LANES
                kern_ref[:, start : start + LANES] = woven[tile, pl.ds(channel, pixels, stride=3), :]
        tokens = bilin_l_ref.shape[0]
        large = grad[small : small + tokens]
        for image in range(1, (grad.shape[0] - small) // tokens):
            large = large + grad[small + image * tokens : small + (image + 1) * tokens]
        table_grad_ref[:first, :] = dot_fine(bilin_s_ref[...], grad[:small], TN) + dot_fine(
            bilin_l_ref[...], large, TN
        )
        table_grad_ref[first : first + 1, :] = jnp.sum(grad, axis=0, keepdims=True)
        table_grad_ref[first + 1 : first + 2, :] = gain
        table_grad_ref[first + 2 : first + 3, :] = shift
        table_grad_ref[first + 3 : first + 6, :] = middle_rows_ref[0:3, :]
        table_grad_ref[first + 6 : first + 7, :] = b_two_ref[...]
        for line in range(b_one_ref.shape[1] // width):
            table_grad_ref[first + 7 + line : first + 8 + line, :] = b_one_ref[
                :, line * width : (line + 1) * width
            ]


def inputs_back(
    heads,
    normed,
    w_qkv,
    inputs,
    back,
    table_state,
    patches,
    bilin_s,
    bilin_l,
    middle_rows,
    bias_one,
    bias_two,
    pixels,
):
    rows, width = inputs.shape
    whole = lambda array: pl.BlockSpec(array.shape, lambda i: (0,) * array.ndim)
    large = rows - patches.shape[0]
    return pl.pallas_call(
        inputs_back_kernel,
        grid=(3,),
        in_specs=[
            pl.BlockSpec((1, rows, width), lambda i: (i, 0, 0)),
            whole(normed),
            pl.BlockSpec((width, width), lambda i: (0, i)),
            whole(inputs),
            whole(back),
            pl.BlockSpec((1,) + table_state.shape[1:], lambda i: (0, 0, 0)),
            whole(patches),
            whole(bilin_s),
            whole(bilin_l),
            whole(middle_rows),
            whole(bias_one),
            whole(bias_two),
        ],
        out_specs=[
            pl.BlockSpec((width, width), lambda i: (0, i)),
            pl.BlockSpec(table_state.shape[1:], lambda i: (0, 0)),
            pl.BlockSpec((large, width), lambda i: (0, 0)),
            pl.BlockSpec((pixels, 3 * width), lambda i: (0, 0)),
        ],
        out_shape=[
            shape_of(w_qkv.shape, BF),
            shape_of(table_state.shape[1:], F32),
            shape_of((large, width), BF),
            shape_of((pixels, 3 * width), F32),
        ],
        scratch_shapes=[
            pltpu.VMEM((width, rows), BF),
            pltpu.VMEM((rows, width), F32),
            pltpu.VMEM((width // LANES, 3 * pixels, LANES), F32),
        ],
        compiler_params=params(),
        cost_estimate=cost(16e9, 0),
        name="inputs_back",
    )(
        heads,
        normed,
        w_qkv,
        inputs,
        back,
        table_state,
        patches,
        bilin_s,
        bilin_l,
        middle_rows,
        bias_one,
        bias_two,
    )


def base_back_kernel(projected_ref, large_ref, small_ref, kern_ref, out_ref):
    rows, width = large_ref.shape
    large = large_ref[...]
    out = dot_fine(small_ref[...], kern_ref[...], TN)
    for channel in range(3):
        part = slice(channel * width, (channel + 1) * width)
        out_ref[:, part] = (
            dot(projected_ref[:, channel * rows : (channel + 1) * rows], large) + out[:, part]
        ).astype(BF)


def base_back(projected, large, resize_s, kern):
    whole = lambda array: pl.BlockSpec(array.shape, lambda i: (0,) * array.ndim)
    rows, wide = projected.shape[0], kern.shape[1]
    return pl.pallas_call(
        base_back_kernel,
        grid=(1,),
        in_specs=[whole(projected), whole(large), whole(resize_s), whole(kern)],
        out_specs=pl.BlockSpec((rows, wide), lambda i: (0, 0)),
        out_shape=shape_of((rows, wide), BF),
        compiler_params=params(),
        cost_estimate=cost(5e9, 0),
        name="base_back",
    )(projected, large, resize_s, kern)


def adam_values(state, gradient, rate, scalars):
    clipped = gradient * scalars[0]
    first = BETA_ONE * state[1] + (1.0 - BETA_ONE) * clipped
    second = BETA_TWO * state[2] + (1.0 - BETA_TWO) * clipped * clipped
    movement = (first * scalars[1]) / (jnp.sqrt(second * scalars[2]) + ADAM_EPS)
    return state[0] - rate * (movement + DECAY * state[0]), first, second


def adam_kernel(count, scalars_ref, *refs):
    scalars = [scalars_ref[place] for place in range(3)]
    for place in range(count):
        state_ref, gradient_ref = refs[2 * place], refs[2 * place + 1]
        new_ref, moments_ref = refs[2 * count + 2 * place], refs[2 * count + 2 * place + 1]
        new, first, second = adam_values(
            state_ref[...], gradient_ref[...].astype(F32), scalars_ref[3 + place], scalars
        )
        new_ref[...] = new
        moments_ref[0] = first
        moments_ref[1] = second


def adam(scalars, states, gradients, steps):
    in_specs = [pl.BlockSpec(memory_space=pltpu.SMEM)]
    out_specs, out_shapes, operands = [], [], [scalars]
    for state, gradient in zip(states, gradients):
        rows, columns = state.shape[1:]
        part = rows // steps
        in_specs.append(pl.BlockSpec((3, part, columns), lambda i: (0, i, 0)))
        in_specs.append(pl.BlockSpec((part, columns), lambda i: (i, 0)))
        out_specs.append(pl.BlockSpec((part, columns), lambda i: (i, 0)))
        out_specs.append(pl.BlockSpec((2, part, columns), lambda i: (0, i, 0)))
        out_shapes.append(shape_of((rows, columns), F32))
        out_shapes.append(shape_of((2, rows, columns), F32))
        operands += [state, gradient]
    return pl.pallas_call(
        functools.partial(adam_kernel, len(states)),
        grid=(steps,),
        in_specs=in_specs,
        out_specs=out_specs,
        out_shape=out_shapes,
        compiler_params=params(),
        cost_estimate=cost(9e9, 0),
        name="optimizer",
    )(*operands)


class Place:
    def __init__(self):
        self.dp, self.mp = lax.axis_size("dp"), lax.axis_size("mp")
        self.index, self.column = lax.axis_index("dp"), lax.axis_index("mp")
        self.direct = self.mp == 2 and self.dp % 8 == 0
        self.outer = self.dp // 4
        self.z, self.x, self.core = self.index // 4, (self.index // 2) % 2, self.index % 2

    def over_core(self, value):
        return lax.ppermute(value, "dp", [(i, i ^ 1) for i in range(self.dp)])

    def over_x(self, value):
        return lax.ppermute(value, "dp", [(i, i ^ 2) for i in range(self.dp)])

    def over_y(self, value):
        return lax.ppermute(value, "mp", [(0, 1), (1, 0)])

    def along_z(self, value, shift):
        rank = lambda i: ((i // 4 + shift) % self.outer) * 4 + i % 4
        return lax.ppermute(value, "dp", [(i, rank(i)) for i in range(self.dp)])

    def xor_z(self, value, bit):
        return lax.ppermute(value, "dp", [(i, i ^ (4 * bit)) for i in range(self.dp)])


def pick(value, index, axis):
    return lax.dynamic_index_in_dim(value, index, axis, keepdims=False)


def add_low(left, right):
    return (left.astype(F32) + right.astype(F32)).astype(BF)


def assemble_kernel(outer, widths, where_ref, *refs):
    parts, wholes = refs[:8], refs[8:]
    height = parts[0].shape[1]
    z, x, core, y = where_ref[0], where_ref[1], where_ref[2], where_ref[3]
    for place, part in enumerate(parts):
        far_x, far_y, far_core = place & 1, (place >> 1) & 1, place >> 2
        column = y if far_y == 0 else 1 - y
        pair = x if far_x == 0 else 1 - x
        single = core if far_core == 0 else 1 - core
        for slot in range(outer):
            block = lax.rem(z - slot + outer, outer) * 4 + pair * 2 + single
            start = 0
            for whole, width in zip(wholes, widths):
                whole[
                    pl.ds(pl.multiple_of(block * height, 16), height),
                    pl.ds(pl.multiple_of(column * width, LANES), width),
                ] = part[slot, :, start : start + width]
                start += width


def assemble(place, parts, widths):
    outer, height = parts[0].shape[:2]
    where = jnp.stack([place.z, place.x, place.core, place.column]).astype(jnp.int32)
    size = 2 * place.dp * height * sum(widths)
    return pl.pallas_call(
        functools.partial(assemble_kernel, outer, widths),
        in_specs=[pl.BlockSpec(memory_space=pltpu.SMEM)] + [pl.BlockSpec(memory_space=pltpu.VMEM)] * 8,
        out_specs=[pl.BlockSpec(memory_space=pltpu.VMEM)] * len(widths),
        out_shape=[shape_of((place.dp * height, 2 * width), BF) for width in widths],
        compiler_params=params(),
        cost_estimate=cost(0, 4 * size),
        name="assemble",
    )(where, *parts)


def gather_shards(place, shards):
    if not place.direct:
        return [
            lax.all_gather(lax.all_gather(s, "dp", axis=0, tiled=True), "mp", axis=1, tiled=True)
            for s in shards
        ]
    widths = [s.shape[1] for s in shards]
    own = jnp.concatenate(shards, axis=1) if len(shards) > 1 else shards[0]
    line = jnp.stack([own] + [place.along_z(own, shift) for shift in range(1, place.outer)])
    half = place.outer // 2
    by_x, by_y = place.over_x(line), place.over_y(line)
    corner = jnp.concatenate([place.over_y(by_x[:half]), place.over_x(by_y[half:])], axis=0)
    near = [line, by_x, by_y, corner]
    return assemble(place, near + [place.over_core(part) for part in near], widths)


def scatter_sums(place, grad):
    if not place.direct:
        rows = lax.psum_scatter(grad, "dp", scatter_dimension=0, tiled=True)
        return lax.psum_scatter(rows, "mp", scatter_dimension=1, tiled=True).astype(F32)
    outer, half = place.outer, place.outer // 2
    height, wide = grad.shape[0] // place.dp, grad.shape[1]
    width = wide // 2
    blocks = grad.reshape(outer, 2, 2, height, wide)
    mine = add_low(
        pick(blocks, place.core, 2), place.over_core(pick(blocks, 1 - place.core, 2))
    )
    side = lambda value, column: lax.dynamic_slice_in_dim(
        value, column * width, width, value.ndim - 1
    )
    upper, lower = mine[:half], mine[half:]
    upper = add_low(pick(upper, place.x, 1), place.over_x(pick(upper, 1 - place.x, 1)))
    lower = add_low(side(lower, place.column), place.over_y(side(lower, 1 - place.column)))
    upper = add_low(side(upper, place.column), place.over_y(side(upper, 1 - place.column)))
    lower = add_low(pick(lower, place.x, 1), place.over_x(pick(lower, 1 - place.x, 1)))
    line = jnp.concatenate([upper, lower], axis=0)
    total = pick(line, place.z, 0).astype(F32)
    for shift in range(1, outer):
        total = total + place.along_z(
            pick(line, lax.rem(place.z + shift, outer), 0), shift
        ).astype(F32)
    return total


def sum_everywhere(place, value):
    if not place.direct:
        return lax.psum(value, ("dp", "mp"))
    value = value + place.over_core(value)
    value = value + place.over_x(value)
    value = value + place.over_y(value)
    bit = 1
    while bit < place.outer:
        value = value + place.xor_z(value, bit)
        bit *= 2
    return value


def sum_over_dp(place, partial):
    if not place.direct:
        total = lax.psum(partial, "dp").astype(F32)
        return total, jnp.where(place.index == 0, jnp.sum(total * total), 0.0)
    outer = place.outer
    height, wide = partial.shape[0] // place.dp, partial.shape[1]
    blocks = partial.reshape(outer, 2, 2, height, wide)
    mine = add_low(pick(blocks, place.core, 2), place.over_core(pick(blocks, 1 - place.core, 2)))
    mine = add_low(pick(mine, place.x, 1), place.over_x(pick(mine, 1 - place.x, 1)))
    total = pick(mine, place.z, 0).astype(F32)
    for shift in range(1, outer):
        total = total + place.along_z(
            pick(mine, lax.rem(place.z + shift, outer), 0), shift
        ).astype(F32)
    own = total.astype(BF)
    squares = jnp.sum(total * total)
    line = jnp.zeros((outer, height, wide), BF)
    line = lax.dynamic_update_index_in_dim(line, own, place.z, 0)
    for shift in range(1, outer):
        source = lax.rem(place.z - shift + outer, outer)
        line = lax.dynamic_update_index_in_dim(line, place.along_z(own, shift), source, 0)
    other = place.over_x(line)
    both = jnp.where(
        place.x == 0, jnp.stack([line, other], axis=1), jnp.stack([other, line], axis=1)
    )
    other = place.over_core(both)
    every = jnp.where(
        place.core == 0, jnp.stack([both, other], axis=2), jnp.stack([other, both], axis=2)
    )
    return every.reshape(partial.shape), squares


def body(
    kernel_state,
    qkv_state,
    proj_state,
    fc1_state,
    fc2_state,
    table_state,
    patches_s,
    patches_l,
    resize_s,
    resize_l,
    bilin_s,
    bilin_l,
    cotangent,
    rates,
    step,
):
    place = Place()
    low = lambda state: state[0].astype(BF)
    (w_qkv,) = gather_shards(place, [low(qkv_state)])
    w_proj, w_fc1 = gather_shards(place, [low(proj_state), low(fc1_state)])
    (w_fc2,) = gather_shards(place, [low(fc2_state)])

    images, image_rows = patches_l.shape[0], patches_l.shape[1]
    large_rows = images * image_rows // place.mp
    projected, embed_part, kern_part = resize_forward(
        kernel_state, resize_s, resize_l, patches_l.reshape(images * image_rows, -1)
    )
    if place.direct:
        kern = kern_part + place.over_y(kern_part.astype(BF)).astype(F32)
        parts = embed_part.reshape(place.mp, large_rows, -1)
        embed_large = pick(parts, place.column, 0) + place.over_y(pick(parts, 1 - place.column, 0))
    else:
        kern = lax.psum(kern_part, "mp")
        embed_large = lax.psum_scatter(embed_part, "mp", scatter_dimension=0, tiled=True)
    patches_own = pick(patches_s, place.column, 0)
    first_rows = patches_own.shape[0]

    inputs, normed_one = embed(patches_own, kern, embed_large, bilin_s, bilin_l, table_state)
    qkv_rows = product(normed_one, w_qkv, D)
    attended, logs = attend(qkv_rows, first_rows, image_rows)
    middle, normed_two = merge(inputs, attended, w_proj, table_state)
    bias_one = table_state[0, POS_GRID * POS_GRID + 7 :].reshape(1, -1)
    block_out, feed_grad, grad_fc1, grad_fc2, bias_one_grad, bias_two_grad = feed(
        middle, normed_two, cotangent, w_fc1, w_fc2, bias_one, table_state, D
    )
    own_fc1, own_fc2 = scatter_sums(place, grad_fc1), scatter_sums(place, grad_fc2)
    middle_grad, heads_up, grad_proj, middle_rows = merge_back(
        feed_grad, middle, cotangent, attended, w_proj, table_state
    )
    own_proj = scatter_sums(place, grad_proj)
    head_grads = attend_back(qkv_rows, attended, heads_up, logs, first_rows, image_rows)
    grad_qkv, table_grad, large_grad, kern_grad = inputs_back(
        head_grads,
        normed_one,
        w_qkv,
        inputs,
        middle_grad,
        table_state,
        patches_own,
        bilin_s,
        bilin_l,
        middle_rows,
        bias_one_grad,
        bias_two_grad,
        resize_s.shape[0],
    )
    own_qkv = scatter_sums(place, grad_qkv)
    table_total = sum_everywhere(place, table_grad)
    if place.direct:
        other = place.over_y(large_grad)
        large_all = jnp.where(
            place.column == 0,
            jnp.concatenate([large_grad, other], axis=0),
            jnp.concatenate([other, large_grad], axis=0),
        )
        kern_grad = kern_grad + place.over_y(kern_grad)
    else:
        large_all = lax.all_gather(large_grad, "mp", axis=0, tiled=True)
        kern_grad = lax.psum(kern_grad, "mp")
    base_grad, squares = sum_over_dp(place, base_back(projected, large_all, resize_s, kern_grad))

    owned = (own_qkv, own_proj, own_fc1, own_fc2)
    for piece in owned:
        squares = squares + jnp.sum(piece * piece)
    square_total = sum_everywhere(place, jnp.full((8, LANES), squares, F32))[0, 0]
    grad_norm = jnp.sqrt(square_total + jnp.sum(table_total * table_total))
    clip_level = 0.5 * math.sqrt(3 * BASE * BASE * D + 4 * D * D + 2 * D * FF + TROWS * D)
    factor = clip_level / jnp.maximum(grad_norm, clip_level)
    count = step[0].astype(F32)
    fix_one = 1.0 / (1.0 - jnp.power(BETA_ONE, count))
    fix_two = 1.0 / (1.0 - jnp.power(BETA_TWO, count))
    fixed = jnp.stack([factor, fix_one, fix_two])
    blocks = adam(
        jnp.concatenate([fixed, rates[1:]]),
        (qkv_state, proj_state, fc1_state, fc2_state, table_state),
        owned + (table_total,),
        1,
    )
    kernel_new, kernel_moments = adam(
        jnp.concatenate([fixed, rates[:1]]), (kernel_state,), (base_grad,), kernel_state.shape[1] // 64
    )
    return (block_out, grad_norm, kernel_new, kernel_moments, *blocks)


def solution(mesh):
    placed = (
        P(None, "mp", None),
        P(None, "dp", "mp"),
        P(None, "dp", "mp"),
        P(None, "dp", "mp"),
        P(None, "dp", "mp"),
        P(),
        P("dp", None, None),
        P("dp", None, None),
        P(None, "mp"),
        P(None, "mp"),
        P(),
        P(),
        P(("dp", "mp"), None),
        P(),
        P(),
    )
    return jax.shard_map(
        body,
        mesh=mesh,
        in_specs=placed,
        out_specs=(
            P(("dp", "mp"), None),
            P(),
            P("mp", None),
            P(None, "mp", None),
            P("dp", "mp"),
            P(None, "dp", "mp"),
            P("dp", "mp"),
            P(None, "dp", "mp"),
            P("dp", "mp"),
            P(None, "dp", "mp"),
            P("dp", "mp"),
            P(None, "dp", "mp"),
            P(),
            P(),
        ),
        check_vma=False,
    )
```

time: 1550 us -> 503 us (0.32)
  waiting for transfers between devices: 745 us -> 166 us
  matrix products: 339 us -> 0 us
  local copies, waits for them, and re-layouts: 245 us -> 36.1 us
  Pallas kernels: 0 us -> 172 us
  blocking collectives: 98.5 us -> 0 us
  starting transfers between devices: 4.66 us -> 87.5 us
  other arithmetic: 76.2 us -> 28.3 us
    reduce_scatter x7 -> x0, waiting for transfers between devices: 445 us -> none  [the longest x1 306 us: body(): lax.psum_scatter(part_large, 'mp', scatter_dimension=1, tiled=True)]
    dot_general x108 -> x0, matrix products: 339 us -> none  [the longest x29 92.4 us: matmul(): return jnp.dot(left, right, preferred_element_type=jnp.float32)]
    psum x2 -> x0, waiting for transfers between devices: 200 us -> none  [the longest x1 131 us: body(): lax.psum(kern_large_grad.astype(jnp.bfloat16), 'dp').astype(jnp.float32)]
    pallas_call x0 -> x15, Pallas kernels: none -> 172 us  [the longest x1 33.9 us: feed(): pl.pallas_call(feed_kernel, grid=(hidden // block,), in_specs=[full, full...]
    ppermute x0 -> x89, waiting for transfers between devices: none -> 166 us  [the longest x20 73 us: over_y(): return lax.ppermute(value, 'mp', [(0, 1), (1, 0)])]
    unnamed x23 -> x0, waiting for transfers between devices: 88.2 us -> none
    ppermute x0 -> x89, starting transfers between devices: none -> 87.5 us  [the longest x27 36.6 us: along_z(): return lax.ppermute(value, 'dp', [(i, rank(i)) for i in range(self.dp)])]
    unnamed x94 -> x93, local copies, waits for them, and re-layouts: 75 us -> 11.6 us
  transfers between devices with their start and end apart: 21 -> 89, of which waited for: 9 -> 33; matrix products, arithmetic and copies ran while one was open for 37% -> 11% of each run, Pallas kernels for 0% -> 12%
where the time goes in v1:
time: 503 us; the launch traced here: 499 us
  Pallas kernels  172 us (34%)
  waiting for transfers between devices  166 us (33%)
  starting transfers between devices  87.5 us (17%)
  local copies, waits for them, and re-layouts  36.1 us (7%)
  other arithmetic  28.3 us (6%)
  between operations  8.65 us (2%)
    ppermute x20, waiting for transfers between devices, over_y(): return lax.ppermute(value, 'mp', [(0, 1), (1, 0)])  73 us
    ppermute x18, waiting for transfers between devices, over_x(): return lax.ppermute(value, 'dp', [(i, i ^ 2) for i in range(self.dp)])  46.6 us
    ppermute x27, waiting for transfers between devices, along_z(): return lax.ppermute(value, 'dp', [(i, rank(i)) for i in range(self.dp)])  41.3 us
    ppermute x27, starting transfers between devices, along_z(): return lax.ppermute(value, 'dp', [(i, rank(i)) for i in range(self.dp)])  36.6 us
    pallas_call x1, Pallas kernels, feed(): pl.pallas_call(feed_kernel, grid=(hidden // block,), in_specs=[full, full...  33.9 us
    pallas_call x1, Pallas kernels, attend_back(): pl.pallas_call(functools.partial(attend_back_kernel, first_rows, image_ro...  29.8 us
    ppermute x20, starting transfers between devices, over_y(): return lax.ppermute(value, 'mp', [(0, 1), (1, 0)])  24.7 us
    pallas_call x1, Pallas kernels, attend(): pl.pallas_call(functools.partial(attend_kernel, first_rows, image_rows, c...  18.3 us
  transfers between devices with their start and end apart: 89, of which 33 were waited for; matrix products, arithmetic and copies ran while one was open for 11% of the time, Pallas kernels for 12%

profile of v1, /device:TPU:0, one launch (start us, length us, event | category | flops | bytes accessed | tf_op | source)
XLA Modules:
  0.0 499.0 jit_solution(2819969385514832988)
XLA Ops:
  15.6 9.7 %resize.1 = (bf16[512,192]{1,0:T(8,128)(2,1)}, f32[64,768]{1,0:T(8,128)}, f32[64,2304]{1,0:T(8,128)}) custom-call(f32[3,512,2304]{2,1,0:T(8,128)} %refs_0_.2, f32[64,512]{1,0:T(8,128)} %small_ref.3, f32[2304,512]{1,0:T(8,128)} %large_ref.1, bf16[64,6912]{1,0:T(8,128)(2,1)} %bitcast.236), custom_call_target="tpu_custom_call" | custom-call | flops 8999999488 | tf_op jit(solution)/shard_map/resize/pallas_call | solution.py:129
  54.3 10.1 %collective-permute-done = bf16[64,2304]{1,0:T(8,128)(2,1)S(1)} collective-permute-done((bf16[64,2304]{1,0:T(8,128)(2,1)S(1)}, bf16[64,2304]{1,0:T(8,128)(2,1)S(1)}, u32[]{:S(2)}, u32[]{:S(2)}) %collective-permute-start) | collective-permute-done | bytes 294944 | tf_op jit(solution)/shard_map/ppermute | solution.py:739
  67.5 9.6 %collective-permute-done.28.refs_2_ = bf16[4,192,384]{2,1,0:T(8,128)(2,1)S(1)} collective-permute-done((bf16[4,192,384]{2,1,0:T(8,128)(2,1)S(1)}, bf16[4,192,384]{2,1,0:T(8,128)(2,1)S(1)}, u32[]{:S(2)}, u32[]{:S(2)}) %collective-permute-start.28) | collective-permute-done | bytes 589856 | tf_op jit(solution)/shard_map/ppermute | solution.py:739
  77.6 17.2 %collective-permute-done.7 = bf16[2,48,1152]{2,1,0:T(8,128)(2,1)S(1)} collective-permute-done((bf16[2,48,1152]{2,1,0:T(8,128)(2,1)S(1)}, bf16[2,48,1152]{2,1,0:T(8,128)(2,1)S(1)}, u32[]{:S(2)}, u32[]{:S(2)}) %collective-permute-start.7) | collective-permute-done | bytes 221216 | tf_op jit(solution)/shard_map/ppermute | solution.py:739
  117.4 6.8 %project.1.q_ref.k_ref.v_ref = bf16[816,2304]{1,0:T(8,128)(2,1)} custom-call(bf16[816,768]{1,0:T(8,128)(2,1)} %get-tuple-element.54.left_ref.a_ref, bf16[768,2304]{1,0:T(8,128)(2,1)} %assemble.3.right_ref.w_ref), custom_call_target="tpu_custom_call" | custom-call | flops 7000000000 | tf_op jit(solution)/shard_map/project/pallas_call | solution.py:217
  126.6 18.3 %attend.1 = (bf16[816,768]{1,0:T(8,128)(2,1)}, f32[6,16,816]{2,1,0:T(8,128)}) custom-call(bf16[816,2304]{1,0:T(8,128)(2,1)} %project.1.q_ref.k_ref.v_ref, bf16[816,2304]{1,0:T(8,128)(2,1)} %project.1.q_ref.k_ref.v_ref, bf16[816,2304]{1,0:T(8,128)(2,1)} %project.1.q_ref.k_ref.v_ref), custom_call_target="tpu_custom_call" | custom-call | flops 17999998976 | tf_op jit(solution)/shard_map/attend/pallas_call | solution.py:276
  152.9 5.7 %assemble.4 = (bf16[768,768]{1,0:T(8,128)(2,1)}, bf16[768,3072]{1,0:T(8,128)(2,1)}) custom-call(s32[4]{0:T(128)} %pad_add_fusion.where_ref, bf16[4,48,1920]{2,1,0:T(8,128)(2,1)} %copy-done.6, bf16[4,48,1920]{2,1,0:T(8,128)(2,1)} %copy-done.12, bf16[4,48,1920]{2,1,0:T(8,128)(2,1)} %copy-done.13, bf16[4,48,1920]{2,1,0:T(8,128)(2,1)} %copy-done.14, ...), custom_call_target="tpu_custom_call" | custom-call | bytes 11796480 | tf_op jit(solution)/shard_map/assemble/pallas_call | solution.py:781
  158.6 5.8 %merge.1 = (f32[816,768]{1,0:T(8,128)}, bf16[816,768]{1,0:T(8,128)(2,1)}) custom-call(f32[816,768]{1,0:T(8,128)} %get-tuple-element.53.x_ref, bf16[816,768]{1,0:T(8,128)(2,1)} %get-tuple-element.55.attended_ref.out_ref, bf16[768,768]{1,0:T(8,128)(2,1)} %get-tuple-element.56.w_ref, f32[3,60,768]{2,1,0:T(8,128)} %refs_8_.1), custom_call_target="tpu_custom_call" | custom-call | flops 6000000000 | tf_op jit(solution)/shard_map/merge/pallas_call | solution.py:300
  164.3 33.9 %feed.1 = (f32[816,768]{1,0:T(8,128)}, f32[816,768]{1,0:T(8,128)}, bf16[768,3072]{1,0:T(8,128)(2,1)}, bf16[3072,768]{1,0:T(8,128)(2,1)}, f32[1,3072]{1,0:T(1,128)}, /*index=5*/f32[1,768]{1,0:T(1,128)}) custom-call(f32[816,768]{1,0:T(8,128)} %get-tuple-element.57.middle_ref, bf16[816,768]{1,0:T(8,128)(2,1)} %get-tuple-element.58.a_ref, ...), custom_call_target="tpu_custom_call" | custom-call | flops 33999998976 | tf_op jit(solution)/shard_map/feed/pallas_call | solution.py:365
  198.3 8.8 %merge_back.1 = (f32[816,768]{1,0:T(8,128)}, bf16[816,768]{1,0:T(8,128)(2,1)}, bf16[768,768]{1,0:T(8,128)(2,1)}, f32[8,768]{1,0:T(8,128)}) custom-call(f32[816,768]{1,0:T(8,128)} %get-tuple-element.62.grad_ref, f32[816,768]{1,0:T(8,128)} %get-tuple-element.57.middle_ref, f32[816,768]{1,0:T(8,128)} %cotangent_ref.3, ...), custom_call_target="tpu_custom_call" | custom-call | flops 8999999488 | tf_op jit(solution)/shard_map/merge_back/pallas_call | solution.py:423
  207.0 29.8 %attend_back.1.heads_ref = bf16[3,816,768]{2,1,0:T(8,128)(2,1)} custom-call(bf16[816,2304]{1,0:T(8,128)(2,1)} %project.1.q_ref.k_ref.v_ref, bf16[816,2304]{1,0:T(8,128)(2,1)} %project.1.q_ref.k_ref.v_ref, bf16[816,2304]{1,0:T(8,128)(2,1)} %project.1.q_ref.k_ref.v_ref, bf16[816,768]{1,0:T(8,128)(2,1)} %get-tuple-element.55.attended_ref.out_ref, ...), custom_call_target="tpu_custom_call" | custom-call | flops 30000001024 | tf_op jit(solution)/shard_map/attend_back/pallas_call | solution.py:493
  236.9 16.1 %inputs_back.1 = (bf16[768,2304]{1,0:T(8,128)(2,1)}, f32[60,768]{1,0:T(8,128)}, bf16[32,768]{1,0:T(8,128)(2,1)}, f32[64,2304]{1,0:T(8,128)}) custom-call(bf16[3,816,768]{2,1,0:T(8,128)(2,1)} %attend_back.1.heads_ref, bf16[816,768]{1,0:T(8,128)(2,1)} %get-tuple-element.54.left_ref.a_ref, bf16[768,2304]{1,0:T(8,128)(2,1)} %assemble.3.right_ref.w_ref, ...), custom_call_target="tpu_custom_call" | custom-call | flops 16000000000 | tf_op jit(solution)/shard_map/inputs_back/pallas_call | solution.py:599
  272.5 11.4 %collective-permute-done.36 = f32[64,2304]{1,0:T(8,128)S(1)} collective-permute-done((f32[64,2304]{1,0:T(8,128)S(1)}, f32[64,2304]{1,0:T(8,128)S(1)}, u32[]{:S(2)}, u32[]{:S(2)}) %collective-permute-start.36) | collective-permute-done | bytes 589856 | tf_op jit(solution)/shard_map/ppermute | solution.py:739
  284.8 5.3 %base_back.1 = bf16[512,2304]{1,0:T(8,128)(2,1)} custom-call(bf16[512,192]{1,0:T(8,128)(2,1)} %get-tuple-element.61.projected_ref, bf16[64,768]{1,0:T(8,128)(2,1)} %maximum_select_fusion.2.large_ref, f32[64,512]{1,0:T(8,128)} %small_ref.3, f32[64,2304]{1,0:T(8,128)} %add.341.kern_ref), custom_call_target="tpu_custom_call" | custom-call | flops 5000000000 | tf_op jit(solution)/shard_map/base_back/pallas_call | solution.py:666
  313.1 8.8 %collective-permute-done.45 = bf16[2,2,48,1152]{3,2,0,1:T(8,128)(2,1)S(1)} collective-permute-done((bf16[2,2,48,1152]{3,2,0,1:T(8,128)(2,1)S(1)}, bf16[2,2,48,1152]{3,2,0,1:T(8,128)(2,1)S(1)}, u32[]{:S(2)}, u32[]{:S(2)}) %collective-permute-start.45) | collective-permute-done | bytes 442400 | tf_op jit(solution)/shard_map/ppermute | solution.py:739
  332.7 5.5 %collective-permute-done.38 = bf16[4,32,2304]{2,1,0:T(8,128)(2,1)S(1)} collective-permute-done((bf16[4,32,2304]{2,1,0:T(8,128)(2,1)S(1)}, bf16[4,32,2304]{2,1,0:T(8,128)(2,1)S(1)}, u32[]{:S(2)}, u32[]{:S(2)}) %collective-permute-start.38) | collective-permute-done | bytes 589856 | tf_op jit(solution)/shard_map/ppermute | solution.py:736
  346.3 6.5 %collective-permute-done.40 = bf16[32,2304]{1,0:T(8,128)(2,1)S(1)} collective-permute-done((bf16[32,2304]{1,0:T(8,128)(2,1)S(1)}, bf16[32,2304]{1,0:T(8,128)(2,1)S(1)}, u32[]{:S(2)}, u32[]{:S(2)}) %collective-permute-start.40) | collective-permute-done | bytes 147488 | tf_op jit(solution)/shard_map/ppermute | solution.py:743
  373.4 6.7 %collective-permute-done.85 = bf16[32,2304]{1,0:T(8,128)(2,1)S(1)} collective-permute-done((bf16[32,2304]{1,0:T(8,128)(2,1)}, bf16[32,2304]{1,0:T(8,128)(2,1)S(1)}, u32[]{:S(2)}, u32[]{:S(2)}) %collective-permute-start.85) | collective-permute-done | bytes 147488 | tf_op jit(solution)/shard_map/ppermute | solution.py:743
  389.3 7.2 %collective-permute-done.59 = bf16[2,48,3072]{2,1,0:T(8,128)(2,1)S(1)} collective-permute-done((bf16[2,48,3072]{2,1,0:T(8,128)(2,1)}, bf16[2,48,3072]{2,1,0:T(8,128)(2,1)S(1)}, u32[]{:S(2)}, u32[]{:S(2)}) %collective-permute-start.59) | collective-permute-done | bytes 589856 | tf_op jit(solution)/shard_map/ppermute | solution.py:736
  397.3 10.8 %collective-permute-done.62 = bf16[2,48,1536]{2,1,0:T(8,128)(2,1)S(1)} collective-permute-done((bf16[2,48,1536]{2,1,0:T(8,128)(2,1)S(1)}, bf16[2,48,1536]{2,1,0:T(8,128)(2,1)S(1)}, u32[]{:S(2)}, u32[]{:S(2)}) %collective-permute-start.62) | collective-permute-done | bytes 294944 | tf_op jit(solution)/shard_map/ppermute | solution.py:736
  409.7 6.4 %collective-permute-done.60 = bf16[2,48,1536]{2,1,0:T(8,128)(2,1)S(1)} collective-permute-done((bf16[2,48,1536]{2,1,0:T(8,128)(2,1)S(1)}, bf16[2,48,1536]{2,1,0:T(8,128)(2,1)S(1)}, u32[]{:S(2)}, u32[]{:S(2)}) %collective-permute-start.60) | collective-permute-done | bytes 294944 | tf_op jit(solution)/shard_map/ppermute | solution.py:739
  425.0 5.2 %collective-permute-done.64 = bf16[48,1536]{1,0:T(8,128)(2,1)S(1)} collective-permute-done((bf16[48,1536]{1,0:T(8,128)(2,1)S(1)}, bf16[48,1536]{1,0:T(8,128)(2,1)S(1)}, u32[]{:S(2)}, u32[]{:S(2)}) %collective-permute-start.64) | collective-permute-done | bytes 147488 | tf_op jit(solution)/shard_map/ppermute | solution.py:743
  448.5 12.5 %collective-permute-done.75 = f32[8,128]{1,0:T(8,128)S(1)} collective-permute-done((f32[8,128]{1,0:T(8,128)S(1)}, f32[8,128]{1,0:T(8,128)S(1)}, u32[]{:S(2)}, u32[]{:S(2)}) %collective-permute-start.75) | collective-permute-done | bytes 4128 | tf_op jit(solution)/shard_map/ppermute | solution.py:736
  483.5 14.1 %optimizer.2 = (f32[512,2304]{1,0:T(8,128)}, f32[2,512,2304]{2,1,0:T(8,128)}) custom-call(f32[4]{0:T(128)} %pad_maximum_fusion.6.scalars_ref, f32[3,512,2304]{2,1,0:T(8,128)} %refs_0_.2, bf16[512,2304]{1,0:T(8,128)(2,1)} %bitcast.216), custom_call_target="tpu_custom_call" | custom-call | flops 8999999488 | tf_op jit(solution)/shard_map/optimizer/pallas_call | solution.py:712
  (379 shorter events, 218.3 us)
Async XLA Ops:
  1.7 29.1 %collective-permute-start.2 = (bf16[48,1152]{1,0:T(8,128)(2,1)S(1)}, bf16[48,1152]{1,0:T(8,128)(2,1)S(1)}, u32[]{:S(2)}, u32[]{:S(2)}) collective-permute-start(bf16[48,1152]{1,0:T(8,128)(2,1)S(1)} %slice_bitcast_fusion.1), channel_id=1, source_target_pairs={{0,8},{2,10},{4,12},{6,14},{8,16},{10,18},{12,20},{14,22},{16,24},... | collective-permute-start | bytes 331784 | tf_op jit(solution)/shard_map/ppermute | solution.py:743
  4.8 28.9 %collective-permute-start.3 = (bf16[48,1152]{1,0:T(8,128)(2,1)S(1)}, bf16[48,1152]{1,0:T(8,128)(2,1)S(1)}, u32[]{:S(2)}, u32[]{:S(2)}) collective-permute-start(bf16[48,1152]{1,0:T(8,128)(2,1)S(1)} %slice_bitcast_fusion.1), channel_id=1, source_target_pairs={{0,16},{2,18},{4,20},{6,22},{8,24},{10,26},{12,28},{14,30},{16,0},... | collective-permute-start | bytes 331784 | tf_op jit(solution)/shard_map/ppermute | solution.py:743
  7.3 26.9 %collective-permute-start.4 = (bf16[48,1152]{1,0:T(8,128)(2,1)S(1)}, bf16[48,1152]{1,0:T(8,128)(2,1)S(1)}, u32[]{:S(2)}, u32[]{:S(2)}) collective-permute-start(bf16[48,1152]{1,0:T(8,128)(2,1)S(1)} %slice_bitcast_fusion.1), channel_id=1, source_target_pairs={{0,24},{2,26},{4,28},{6,30},{8,0},{10,2},{12,4},{14,6},{16,8},{18,... | collective-permute-start | bytes 331784 | tf_op jit(solution)/shard_map/ppermute | solution.py:743
  9.7 30.7 %collective-permute-start.24 = (bf16[192,384]{1,0:T(8,128)(2,1)S(1)}, bf16[192,384]{1,0:T(8,128)(2,1)S(1)}, u32[]{:S(2)}, u32[]{:S(2)}) collective-permute-start(bf16[192,384]{1,0:T(8,128)(2,1)S(1)} %slice_bitcast_fusion.2), channel_id=1, source_target_pairs={{0,8},{2,10},{4,12},{6,14},{8,16},{10,18},{12,20},{14,22},{16,24},... | collective-permute-start | bytes 442376 | tf_op jit(solution)/shard_map/ppermute | solution.py:743
  10.4 33.1 %collective-permute-start.25 = (bf16[192,384]{1,0:T(8,128)(2,1)S(1)}, bf16[192,384]{1,0:T(8,128)(2,1)S(1)}, u32[]{:S(2)}, u32[]{:S(2)}) collective-permute-start(bf16[192,384]{1,0:T(8,128)(2,1)S(1)} %slice_bitcast_fusion.2), channel_id=1, source_target_pairs={{0,16},{2,18},{4,20},{6,22},{8,24},{10,26},{12,28},{14,30},{16,0},... | collective-permute-start | bytes 442376 | tf_op jit(solution)/shard_map/ppermute | solution.py:743
  52.0 25.0 %collective-permute-start.28 = (bf16[4,192,384]{2,1,0:T(8,128)(2,1)S(1)}, bf16[4,192,384]{2,1,0:T(8,128)(2,1)S(1)}, u32[]{:S(2)}, u32[]{:S(2)}) collective-permute-start(bf16[4,192,384]{2,1,0:T(8,128)(2,1)S(1)} %pad_maximum_fusion.3.refs_0_), channel_id=1, source_target_pairs={{0,1},{1,0},{2,3},{3,2},{4,5},{5,4},{6,7},{7,6},{8,9},{9,8},{10,11... | collective-permute-start | bytes 1769480 | tf_op jit(solution)/shard_map/ppermute | solution.py:739
  53.7 42.8 %collective-permute-start.16 = (bf16[4,48,1920]{2,1,0:T(8,128)(2,1)S(1)}, bf16[4,48,1920]{2,1,0:T(8,128)(2,1)S(1)}, u32[]{:S(2)}, u32[]{:S(2)}) collective-permute-start(bf16[4,48,1920]{2,1,0:T(8,128)(2,1)S(1)} %pad_maximum_fusion.2.refs_0_), channel_id=1, source_target_pairs={{0,4},{2,6},{4,0},{6,2},{8,12},{10,14},{12,8},{14,10},{16,20},{18,... | collective-permute-start | bytes 2211848 | tf_op jit(solution)/shard_map/ppermute | solution.py:736
  64.4 32.7 %collective-permute-start.17 = (bf16[4,48,1920]{2,1,0:T(8,128)(2,1)S(1)}, bf16[4,48,1920]{2,1,0:T(8,128)(2,1)S(1)}, u32[]{:S(2)}, u32[]{:S(2)}) collective-permute-start(bf16[4,48,1920]{2,1,0:T(8,128)(2,1)S(1)} %pad_maximum_fusion.2.refs_0_), channel_id=1, source_target_pairs={{0,1},{1,0},{2,3},{3,2},{4,5},{5,4},{6,7},{7,6},{8,9},{9,8},{10,11... | collective-permute-start | bytes 2211848 | tf_op jit(solution)/shard_map/ppermute | solution.py:739
  65.9 28.9 %collective-permute-start.7 = (bf16[2,48,1152]{2,1,0:T(8,128)(2,1)S(1)}, bf16[2,48,1152]{2,1,0:T(8,128)(2,1)S(1)}, u32[]{:S(2)}, u32[]{:S(2)}) collective-permute-start(bf16[2,48,1152]{2,1,0:T(8,128)(2,1)S(1)} %slice.90), channel_id=1, source_target_pairs={{0,1},{1,0},{2,3},{3,2},{4,5},{5,4},{6,7},{7,6},{8,9},{9,8},{10,11... | collective-permute-start | bytes 663560 | tf_op jit(solution)/shard_map/ppermute | solution.py:739
  67.4 43.3 %collective-permute-start.9 = (bf16[4,48,1152]{2,1,0:T(8,128)(2,1)S(1)}, bf16[4,48,1152]{2,1,0:T(8,128)(2,1)S(1)}, u32[]{:S(2)}, u32[]{:S(2)}) collective-permute-start(bf16[4,48,1152]{2,1,0:T(8,128)(2,1)S(1)} %pad_maximum_fusion.4.refs_0_), channel_id=1, source_target_pairs={{0,2},{2,0},{4,6},{6,4},{8,10},{10,8},{12,14},{14,12},{16,18},{18,... | collective-permute-start | bytes 1327112 | tf_op jit(solution)/shard_map/ppermute | solution.py:733
  124.2 26.5 %collective-permute-start.20 = (bf16[4,48,1920]{2,1,0:T(8,128)(2,1)S(1)}, bf16[4,48,1920]{2,1,0:T(8,128)(2,1)S(1)}, u32[]{:S(2)}, u32[]{:S(2)}) collective-permute-start(bf16[4,48,1920]{2,1,0:T(8,128)(2,1)S(1)} %pad_maximum_fusion.2.refs_0_), channel_id=1, source_target_pairs={{0,2},{2,0},{4,6},{6,4},{8,10},{10,8},{12,14},{14,12},{16,18},{18,... | collective-permute-start | bytes 2211848 | tf_op jit(solution)/shard_map/ppermute | solution.py:733
  125.3 25.4 %collective-permute-start.21 = (bf16[4,48,1920]{2,1,0:T(8,128)(2,1)S(1)}, bf16[4,48,1920]{2,1,0:T(8,128)(2,1)S(1)}, u32[]{:S(2)}, u32[]{:S(2)}) collective-permute-start(bf16[4,48,1920]{2,1,0:T(8,128)(2,1)S(1)} %collective-permute-done.16.refs_1_), channel_id=1, source_target_pairs={{0,2},{2,0},{4,6},{6,4},{8,10},{10,8},{12,14},{14,12},{16,18},{18,... | collective-permute-start | bytes 2211848 | tf_op jit(solution)/shard_map/ppermute | solution.py:733
  125.9 24.8 %collective-permute-start.22 = (bf16[4,48,1920]{2,1,0:T(8,128)(2,1)S(1)}, bf16[4,48,1920]{2,1,0:T(8,128)(2,1)S(1)}, u32[]{:S(2)}, u32[]{:S(2)}) collective-permute-start(bf16[4,48,1920]{2,1,0:T(8,128)(2,1)S(1)} %collective-permute-done.17.refs_2_), channel_id=1, source_target_pairs={{0,2},{2,0},{4,6},{6,4},{8,10},{10,8},{12,14},{14,12},{16,18},{18,... | collective-permute-start | bytes 2211848 | tf_op jit(solution)/shard_map/ppermute | solution.py:733
  126.5 24.2 %collective-permute-start.23 = (bf16[4,48,1920]{2,1,0:T(8,128)(2,1)S(1)}, bf16[4,48,1920]{2,1,0:T(8,128)(2,1)S(1)}, u32[]{:S(2)}, u32[]{:S(2)}) collective-permute-start(bf16[4,48,1920]{2,1,0:T(8,128)(2,1)S(1)} %constant_dynamic-update-slice_fusion.2.refs_3_), channel_id=1, source_target_pairs={{0,2},{2,0},{4,6},{6,4},{8,10},{10,8},{12,14},{14,12},{16,18},{18,... | collective-permute-start | bytes 2211848 | tf_op jit(solution)/shard_map/ppermute | solution.py:733
  267.8 40.1 %collective-permute-start.42 = (bf16[4,2,48,2304]{3,2,0,1:T(8,128)(2,1)}, bf16[4,2,48,2304]{3,2,0,1:T(8,128)(2,1)}, u32[]{:S(2)}, u32[]{:S(2)}) collective-permute-start(bf16[4,2,48,2304]{3,2,0,1:T(8,128)(2,1)} %bitcast.198), channel_id=1, source_target_pairs={{0,2},{2,0},{4,6},{6,4},{8,10},{10,8},{12,14},{14,12},{16,18},{18,... | collective-permute-start | bytes 5308424 | tf_op jit(solution)/shard_map/ppermute | solution.py:733
  270.0 32.3 %collective-permute-start.82 = (f32[60,768]{1,0:T(8,128)S(1)}, f32[60,768]{1,0:T(8,128)}, u32[]{:S(2)}, u32[]{:S(2)}) collective-permute-start(f32[60,768]{1,0:T(8,128)S(1)} %add.407), channel_id=1, source_target_pairs={{0,8},{2,10},{4,12},{6,14},{8,0},{10,2},{12,4},{14,6},{16,24},{18,... | collective-permute-start | bytes 552968 | tf_op jit(solution)/shard_map/ppermute | solution.py:746
  304.1 25.2 %collective-permute-start.58 = (bf16[4,2,48,3072]{3,2,0,1:T(8,128)(2,1)S(1)}, bf16[4,2,48,3072]{3,2,0,1:T(8,128)(2,1)S(1)}, u32[]{:S(2)}, u32[]{:S(2)}) collective-permute-start(bf16[4,2,48,3072]{3,2,0,1:T(8,128)(2,1)S(1)} %bitcast.214), channel_id=1, source_target_pairs={{0,2},{2,0},{4,6},{6,4},{8,10},{10,8},{12,14},{14,12},{16,18},{18,... | collective-permute-start | bytes 7077896 | tf_op jit(solution)/shard_map/ppermute | solution.py:733
  304.6 142.6 %collective-permute-start.83 = (f32[60,768]{1,0:T(8,128)S(1)}, f32[60,768]{1,0:T(8,128)S(1)}, u32[]{:S(2)}, u32[]{:S(2)}) collective-permute-start(f32[60,768]{1,0:T(8,128)S(1)} %add.408), channel_id=1, source_target_pairs={{0,16},{2,18},{4,20},{6,22},{8,24},{10,26},{12,28},{14,30},{16,0},... | collective-permute-start | bytes 552968 | tf_op jit(solution)/shard_map/ppermute | solution.py:746
  329.2 51.4 %collective-permute-start.69 = (bf16[2,2,192,384]{3,2,0,1:T(8,128)(2,1)}, bf16[2,2,192,384]{3,2,0,1:T(8,128)(2,1)}, u32[]{:S(2)}, u32[]{:S(2)}) collective-permute-start(bf16[2,2,192,384]{3,2,0,1:T(8,128)(2,1)} %constant_dynamic-slice_fusion), channel_id=1, source_target_pairs={{0,1},{1,0},{2,3},{3,2},{4,5},{5,4},{6,7},{7,6},{8,9},{9,8},{10,11... | collective-permute-start | bytes 1769480 | tf_op jit(solution)/shard_map/ppermute | solution.py:739
  358.6 25.1 %collective-permute-start.67 = (bf16[2,192,768]{2,1,0:T(8,128)(2,1)}, bf16[2,192,768]{2,1,0:T(8,128)(2,1)}, u32[]{:S(2)}, u32[]{:S(2)}) collective-permute-start(bf16[2,192,768]{2,1,0:T(8,128)(2,1)} %dynamic-slice_bitcast_fusion), channel_id=1, source_target_pairs={{0,4},{2,6},{4,0},{6,2},{8,12},{10,14},{12,8},{14,10},{16,20},{18,... | collective-permute-start | bytes 1769480 | tf_op jit(solution)/shard_map/ppermute | solution.py:736
  362.1 24.3 %collective-permute-start.61 = (bf16[2,2,48,1536]{3,2,0,1:T(8,128)(2,1)}, bf16[2,2,48,1536]{3,2,0,1:T(8,128)(2,1)}, u32[]{:S(2)}, u32[]{:S(2)}) collective-permute-start(bf16[2,2,48,1536]{3,2,0,1:T(8,128)(2,1)} %constant_dynamic-slice_fusion.4), channel_id=1, source_target_pairs={{0,1},{1,0},{2,3},{3,2},{4,5},{5,4},{6,7},{7,6},{8,9},{9,8},{10,11... | collective-permute-start | bytes 1769480 | tf_op jit(solution)/shard_map/ppermute | solution.py:739
  380.7 63.5 %collective-permute-start.86 = (bf16[32,2304]{1,0:T(8,128)(2,1)}, bf16[32,2304]{1,0:T(8,128)(2,1)}, u32[]{:S(2)}, u32[]{:S(2)}) collective-permute-start(bf16[32,2304]{1,0:T(8,128)(2,1)} %get-tuple-element.117), channel_id=1, source_target_pairs={{0,24},{2,26},{4,28},{6,30},{8,0},{10,2},{12,4},{14,6},{16,8},{18,... | collective-permute-start | bytes 442376 | tf_op jit(solution)/shard_map/ppermute | solution.py:743
  383.7 32.7 %collective-permute-start.70 = (bf16[2,192,384]{2,1,0:T(8,128)(2,1)S(1)}, bf16[2,192,384]{2,1,0:T(8,128)(2,1)S(1)}, u32[]{:S(2)}, u32[]{:S(2)}) collective-permute-start(bf16[2,192,384]{2,1,0:T(8,128)(2,1)S(1)} %dynamic-slice_bitcast_fusion.4), channel_id=1, source_target_pairs={{0,4},{2,6},{4,0},{6,2},{8,12},{10,14},{12,8},{14,10},{16,20},{18,... | collective-permute-start | bytes 884744 | tf_op jit(solution)/shard_map/ppermute | solution.py:736
  386.5 30.1 %collective-permute-start.68 = (bf16[2,192,384]{2,1,0:T(8,128)(2,1)S(1)}, bf16[2,192,384]{2,1,0:T(8,128)(2,1)S(1)}, u32[]{:S(2)}, u32[]{:S(2)}) collective-permute-start(bf16[2,192,384]{2,1,0:T(8,128)(2,1)S(1)} %constant_dynamic-slice_fusion.1), channel_id=1, source_target_pairs={{0,1},{1,0},{2,3},{3,2},{4,5},{5,4},{6,7},{7,6},{8,9},{9,8},{10,11... | collective-permute-start | bytes 884744 | tf_op jit(solution)/shard_map/ppermute | solution.py:739
  (108 other events, 1362.4 us)

commit v2 on v1

v2 whole, which is shorter than its diff:
```python
import functools
import math

import jax
import jax.numpy as jnp
from jax import lax
from jax.experimental import pallas as pl
from jax.experimental.pallas import tpu as pltpu
from jax.sharding import PartitionSpec as P

D = 768
HEADS = 12
HEAD_DIM = 64
FF = 3072
BASE = 32
POS_GRID = 7
GRID_S = 28
GRID_L = 4
TROWS = 60

NORM_EPS = 1e-06
BETA_ONE = 0.5
BETA_TWO = 0.5
DECAY = 0.05
ADAM_EPS = 1e-08
MASKED = -1e30
LOG2E = 1.4426950408889634
LANES = 128
MIB = 2**20

BF = jnp.bfloat16
F32 = jnp.float32
NN = (((1,), (0,)), ((), ()))
NT = (((1,), (1,)), ((), ()))
TN = (((0,), (0,)), ((), ()))


def shape_of(dims, dtype):
    return jax.ShapeDtypeStruct(dims, dtype)


def params(mib=56):
    return pltpu.CompilerParams(vmem_limit_bytes=mib * MIB)


def cost(flops, moved):
    return pl.CostEstimate(flops=int(flops), bytes_accessed=int(moved), transcendentals=0)


def dot(left, right, dims=NN):
    return lax.dot_general(left, right, dims, preferred_element_type=F32)


def run(kernel, operands, out_shape, deps=(), in_specs=None, name=None, micros=1, mib=56, **rest):
    count, skip = len(operands), len(deps)

    def inner(*refs):
        kernel(*refs[:count], *refs[count + skip :])

    if in_specs is None:
        in_specs = [pl.BlockSpec(memory_space=pltpu.VMEM)] * count
    return pl.pallas_call(
        inner,
        in_specs=list(in_specs) + [pl.BlockSpec(memory_space=pl.ANY)] * skip,
        out_shape=out_shape,
        compiler_params=params(mib),
        cost_estimate=cost(micros * 1e8, 0),
        name=name,
        **rest,
    )(*operands, *deps)


def whole(array):
    return pl.BlockSpec(array.shape, lambda *i: (0,) * len(array.shape))


SCALARS = pl.BlockSpec(memory_space=pltpu.SMEM)
INSIDE = pl.BlockSpec(memory_space=pltpu.VMEM)


def first_state(state):
    return pl.BlockSpec((1,) + state.shape[1:], lambda *i: (0, 0, 0))


def halves(value):
    high = value.astype(BF)
    return high, (value - high.astype(F32)).astype(BF)


def dot_fine(left, right, dims=NN):
    left_high, left_low = halves(left)
    right_high, right_low = halves(right)
    return dot(left_high, right_high, dims) + (
        dot(left_high, right_low, dims) + dot(left_low, right_high, dims)
    )


def norm_forward(inputs):
    centered = inputs - jnp.mean(inputs, axis=-1, keepdims=True)
    inverse = lax.rsqrt(jnp.mean(centered * centered, axis=-1, keepdims=True) + NORM_EPS)
    return centered * inverse, inverse


def norm_backward(upstream, normalized, inverse, gain_row):
    scaled = upstream * gain_row
    inner = jnp.mean(scaled * normalized, axis=-1, keepdims=True)
    result = inverse * (scaled - jnp.mean(scaled, axis=-1, keepdims=True) - normalized * inner)
    return (
        result,
        jnp.sum(upstream * normalized, axis=0, keepdims=True),
        jnp.sum(upstream, axis=0, keepdims=True),
    )


def resize_kernel(
    base_ref, small_ref, large_ref, patch_ref, projected_ref, embed_ref, kern_ref, turned, pixels_ref
):
    rows = embed_ref.shape[0]

    @pl.when(pl.program_id(0) == 0)
    def _():
        embed_ref[...] = jnp.zeros_like(embed_ref)
        kern_ref[...] = jnp.zeros_like(kern_ref)
        count = large_ref.shape[0]
        for start in range(0, rows, LANES):
            size = min(LANES, rows - start)
            patch = patch_ref[start : start + size, :].astype(F32)
            if size < LANES:
                patch = jnp.concatenate(
                    [patch, jnp.zeros((LANES - size, patch.shape[1]), F32)], axis=0
                )
            turned[...] = patch.T
            for channel in range(3):
                across = turned[pl.ds(channel, count, stride=3), :].T
                pixels_ref[channel * rows + start : channel * rows + start + size, :] = across[
                    :size
                ].astype(BF)

    base = base_ref[0]
    width = base.shape[1] // 3
    large_high, large_low = halves(large_ref[...])
    pixels = pixels_ref[...]
    projected = dot(pixels, large_high) + dot(pixels, large_low)
    kern_ref[...] += dot_fine(small_ref[...], base)
    total = embed_ref[...]
    for channel in range(3):
        part = projected[channel * rows : (channel + 1) * rows]
        projected_ref[channel] = part.astype(BF)
        total += dot_fine(part, base[:, channel * width : (channel + 1) * width])
    embed_ref[...] = total


def resize_forward(kernel_state, resize_s, resize_l, patches):
    base_rows, wide = kernel_state.shape[1:]
    count = base_rows // LANES
    rows = patches.shape[0]
    columns = 3 * rows
    return pl.pallas_call(
        resize_kernel,
        grid=(count,),
        in_specs=[
            pl.BlockSpec((1, LANES, wide), lambda i: (0, i, 0)),
            pl.BlockSpec((resize_s.shape[0], LANES), lambda i: (0, i)),
            pl.BlockSpec((resize_l.shape[0], LANES), lambda i: (0, i)),
            pl.BlockSpec(patches.shape, lambda i: (0, 0)),
        ],
        out_specs=[
            pl.BlockSpec((3, rows, LANES), lambda i: (0, 0, i)),
            pl.BlockSpec((rows, wide // 3), lambda i: (0, 0)),
            pl.BlockSpec((resize_s.shape[0], wide), lambda i: (0, 0)),
        ],
        out_shape=[
            shape_of((3, rows, base_rows), BF),
            shape_of((rows, wide // 3), F32),
            shape_of((resize_s.shape[0], wide), F32),
        ],
        scratch_shapes=[
            pltpu.VMEM((patches.shape[1], LANES), F32),
            pltpu.VMEM((columns, resize_l.shape[0]), BF),
        ],
        compiler_params=params(),
        cost_estimate=cost(9e8, 0),
        name="resize",
    )(kernel_state, resize_s, resize_l, patches)


def embed_kernel(
    patch_ref, kern_ref, large_ref, bilin_s_ref, bilin_l_ref, table_ref, x_ref, a_ref, woven
):
    table = table_ref[0]
    first = POS_GRID * POS_GRID
    pixels = kern_ref.shape[0]
    width = table.shape[1]
    tiles = width // LANES
    for channel in range(3):
        for tile in range(tiles):
            start = channel * width + tile * LANES
            woven[tile, pl.ds(channel, pixels, stride=3), :] = kern_ref[:, start : start + LANES]
    kern = jnp.concatenate([woven[tile].astype(BF) for tile in range(tiles)], axis=1)
    grid_rows = table[:first]
    bias = table[first : first + 1]
    small = patch_ref.shape[0]
    x_ref[:small, :] = (
        dot(patch_ref[...], kern) + dot_fine(bilin_s_ref[...], grid_rows) + bias
    )
    tokens = bilin_l_ref.shape[0]
    placed = dot_fine(bilin_l_ref[...], grid_rows) + bias
    for image in range(large_ref.shape[0] // tokens):
        part = slice(image * tokens, (image + 1) * tokens)
        x_ref[small + image * tokens : small + (image + 1) * tokens, :] = large_ref[part, :] + placed
    normal, _ = norm_forward(x_ref[...])
    a_ref[...] = (normal * table[first + 1 : first + 2] + table[first + 2 : first + 3]).astype(BF)


def embed(patches, kern, large, bilin_s, bilin_l, table_state):
    rows = patches.shape[0] + large.shape[0]
    width = table_state.shape[2]
    return run(
        embed_kernel,
        (patches, kern, large, bilin_s, bilin_l, table_state),
        [shape_of((rows, width), F32), shape_of((rows, width), BF)],
        (),
        [INSIDE] * 5 + [first_state(table_state)],
        grid=(1,),
        out_specs=[INSIDE] * 2,
        scratch_shapes=[pltpu.VMEM((width // LANES, patches.shape[1], LANES), F32)],
        name="embed",
        micros=5,
    )


def product_kernel(left_ref, right_ref, out_ref):
    out_ref[...] = dot(left_ref[...], right_ref[...]).astype(BF)


def product(left, right, block):
    rows, depth = left.shape
    columns = right.shape[1]
    return pl.pallas_call(
        product_kernel,
        grid=(columns // block,),
        in_specs=[
            pl.BlockSpec((rows, depth), lambda i: (0, 0)),
            pl.BlockSpec((depth, block), lambda i: (0, i)),
        ],
        out_specs=pl.BlockSpec((rows, block), lambda i: (0, i)),
        out_shape=shape_of((rows, columns), BF),
        compiler_params=params(),
        cost_estimate=cost(7e8, 0),
        name="project",
    )(left, right)


def image_features(rows, first_rows, image_rows):
    row = lax.broadcasted_iota(jnp.int32, (rows, LANES), 0)
    lane = lax.broadcasted_iota(jnp.int32, (rows, LANES), 1) % HEAD_DIM
    label = jnp.where(row < first_rows, 0, 1 + (row - first_rows) // image_rows)
    count = 1 + (rows - first_rows) // image_rows
    own = label == lane
    query = jnp.where(own | (lane >= count), 0.0, MASKED).astype(BF)
    return query, jnp.where(own, 1.0, 0.0).astype(BF)


def attend_kernel(first_rows, image_rows, chunks, q_ref, k_ref, v_ref, out_ref, log_ref):
    rows = q_ref.shape[0]
    query_mark, key_mark = image_features(rows, first_rows, image_rows)
    low = lax.broadcasted_iota(jnp.int32, (rows, LANES), 1) < HEAD_DIM
    step = rows // chunks
    queries = q_ref[...] * jnp.asarray(HEAD_DIM**-0.5, BF)
    keys, values = k_ref[...], v_ref[...]
    ones = jnp.ones((rows, LANES), BF)
    results = []
    for head in range(2):
        mine = low if head == 0 else ~low
        query = jnp.where(mine, queries, query_mark)
        key = jnp.where(mine, keys, key_mark)
        value = jnp.where(mine, values, ones)
        outs, logs = [], []
        for chunk in range(chunks):
            scores = dot(query[chunk * step : (chunk + 1) * step], key, NT)
            largest = jnp.max(scores, axis=1, keepdims=True)
            probs = jnp.exp2(scores * LOG2E - largest * LOG2E)
            summed = dot(probs.astype(BF), value)
            rolled = pltpu.roll(summed, HEAD_DIM, 1)
            outs.append(summed / rolled)
            logs.append(largest * LOG2E + jnp.log2(jnp.where(mine[:step], rolled, summed)))
        results.append(jnp.concatenate(outs, axis=0))
        log_ref[0, 8 * head : 8 * head + 8, :] = jnp.concatenate(logs, axis=0).T[:8]
    out_ref[...] = jnp.where(low, results[0], results[1]).astype(BF)


def attend(qkv, first_rows, image_rows, start, count, deps=()):
    rows, wide = qkv.shape
    pairs = wide // 3 // LANES
    chunks = 3 if rows % 48 == 0 else 1
    part = lambda offset: pl.BlockSpec((rows, LANES), lambda i: (0, offset + i))
    return run(
        functools.partial(attend_kernel, first_rows, image_rows, chunks),
        (qkv, qkv, qkv),
        [shape_of((rows, count * LANES), BF), shape_of((count, 16, rows), F32)],
        deps,
        [part(start), part(pairs + start), part(2 * pairs + start)],
        grid=(count,),
        out_specs=[part(0), pl.BlockSpec((1, 16, rows), lambda i: (i, 0, 0))],
        name="attend",
        micros=3 * count,
    )


def merge_kernel(x_ref, w_ref, table_ref, *refs):
    attended, (middle_ref, a_ref) = refs[:-2], refs[-2:]
    first = POS_GRID * POS_GRID
    table = table_ref[0]
    middle = x_ref[...] + table[first + 5 : first + 6]
    start = 0
    for part in attended:
        size = part.shape[1]
        middle = middle + dot(part[...], w_ref[start : start + size, :])
        start += size
    middle_ref[...] = middle
    normal, _ = norm_forward(middle)
    a_ref[...] = (normal * table[first + 3 : first + 4] + table[first + 4 : first + 5]).astype(BF)


def merge(inputs, attended, w_proj, table_state, deps=()):
    rows, width = inputs.shape
    return run(
        merge_kernel,
        (inputs, w_proj, table_state, *attended),
        [shape_of((rows, width), F32), shape_of((rows, width), BF)],
        deps,
        [INSIDE, INSIDE, first_state(table_state)] + [INSIDE] * len(attended),
        grid=(1,),
        out_specs=[INSIDE] * 2,
        name="merge",
        micros=6,
    )


def feed_kernel(
    middle_ref,
    cotangent_ref,
    a_ref,
    w_one_ref,
    w_two_ref,
    bias_ref,
    table_ref,
    out_ref,
    grad_ref,
    g_one_ref,
    g_two_ref,
    b_one_ref,
    b_two_ref,
    turned,
    upstream,
):
    place = pl.program_id(0)

    @pl.when(place == 0)
    def _():
        first = POS_GRID * POS_GRID
        turned[...] = a_ref[...].T
        low = cotangent_ref[...].astype(BF)
        upstream[...] = low
        out_ref[...] = middle_ref[...] + table_ref[0][first + 6 : first + 7]
        grad_ref[...] = jnp.zeros_like(grad_ref)
        b_two_ref[...] = jnp.sum(low.astype(F32), axis=0, keepdims=True)

    w_one, w_two, dz = w_one_ref[...], w_two_ref[...], upstream[...]
    hidden = dot(a_ref[...], w_one) + bias_ref[...]
    phi = 0.5 * (1.0 + lax.erf(hidden * 0.7071067811865476))
    active = (hidden * phi).astype(BF)
    slope = phi + hidden * jnp.exp(-0.5 * hidden * hidden) * 0.3989422804014327
    change = dot(dz, w_two, NT) * slope
    b_one_ref[...] = jnp.sum(change, axis=0, keepdims=True)
    change = change.astype(BF)
    out_ref[...] += dot(active, w_two)
    grad_ref[...] += dot(change, w_one, NT)
    g_one_ref[...] = dot(turned[...], change).astype(BF)
    g_two_ref[...] = dot(active, dz, TN).astype(BF)


def feed(middle, cotangent, normed, w_one, w_two, bias_one, table_state):
    rows, width = normed.shape
    hidden = w_one.shape[1]
    block = D
    across = pl.BlockSpec((width, block), lambda i: (0, i))
    down = pl.BlockSpec((block, width), lambda i: (i, 0))
    line = pl.BlockSpec((1, block), lambda i: (0, i))
    return run(
        feed_kernel,
        (middle, cotangent, normed, w_one, w_two, bias_one, table_state),
        [
            shape_of((rows, width), F32),
            shape_of((rows, width), F32),
            shape_of((width, hidden), BF),
            shape_of((hidden, width), BF),
            shape_of((1, hidden), F32),
            shape_of((1, width), F32),
        ],
        (),
        [INSIDE, INSIDE, INSIDE, across, down, line, first_state(table_state)],
        grid=(hidden // block,),
        out_specs=[INSIDE, INSIDE, across, down, line, INSIDE],
        scratch_shapes=[pltpu.VMEM((width, rows), BF), pltpu.VMEM((rows, width), BF)],
        name="feed",
        micros=9 * (hidden // block),
        mib=60,
    )


def merge_back_kernel(count, grad_ref, middle_ref, cotangent_ref, w_ref, table_ref, *refs):
    attended = refs[:count]
    back_ref, heads_ref, rows_ref, g_ref = refs[count:]
    first = POS_GRID * POS_GRID
    normal, inverse = norm_forward(middle_ref[...])
    change, gain, shift = norm_backward(
        grad_ref[...], normal, inverse, table_ref[0][first + 3 : first + 4]
    )
    back = cotangent_ref[...] + change
    back_ref[...] = back
    low = back.astype(BF)
    heads_ref[...] = dot(low, w_ref[...], NT).astype(BF)
    start = 0
    for part in attended:
        size = part.shape[1]
        g_ref[start : start + size, :] = dot(part[...], low, TN).astype(BF)
        start += size
    rows_ref[0:1, :] = gain
    rows_ref[1:2, :] = shift
    rows_ref[2:3, :] = jnp.sum(low.astype(F32), axis=0, keepdims=True)


def merge_back(grad, middle, cotangent, attended, w_proj, table_state):
    rows, width = middle.shape
    return run(
        functools.partial(merge_back_kernel, len(attended)),
        (grad, middle, cotangent, w_proj, table_state, *attended),
        [
            shape_of((rows, width), F32),
            shape_of((rows, width), BF),
            shape_of((8, width), F32),
            shape_of(w_proj.shape, BF),
        ],
        (),
        [INSIDE, INSIDE, INSIDE, INSIDE, first_state(table_state)] + [INSIDE] * len(attended),
        grid=(1,),
        out_specs=[INSIDE] * 4,
        name="merge_back",
        micros=9,
    )


def attend_back_kernel(
    first_rows, image_rows, chunks, q_ref, k_ref, v_ref, out_ref, up_ref, log_ref, grad_ref
):
    rows = q_ref.shape[0]
    query_mark, key_mark = image_features(rows, first_rows, image_rows)
    low = lax.broadcasted_iota(jnp.int32, (rows, LANES), 1) < HEAD_DIM
    step = rows // chunks
    queries = q_ref[...] * jnp.asarray(HEAD_DIM**-0.5, BF)
    keys, values, up = k_ref[...], v_ref[...], up_ref[...]
    overlap = (out_ref[...].astype(F32) * up.astype(F32)).T
    zeros = jnp.zeros((rows, LANES), BF)
    grads = ([], [], [])
    for head in range(2):
        mine = low if head == 0 else ~low
        query = jnp.where(mine, queries, query_mark)
        key = jnp.where(mine, keys, key_mark)
        value = jnp.where(mine, values, zeros)
        inner = jnp.sum(overlap[HEAD_DIM * head : HEAD_DIM * (head + 1)], axis=0, keepdims=True)
        totals = log_ref[0, 8 * head : 8 * head + 1, :]
        query_grad = jnp.zeros((rows, LANES), F32)
        key_grads, value_grads = [], []
        for chunk in range(chunks):
            part = slice(chunk * step, (chunk + 1) * step)
            scores = dot(key[part], query, NT)
            probs = jnp.exp2(scores * LOG2E - totals)
            value_grads.append(dot(probs.astype(BF), up))
            change = (probs * (dot(value[part], up, NT) - inner)).astype(BF)
            key_grads.append(dot(change, queries))
            query_grad = query_grad + dot(change, keys[part], TN)
        grads[0].append(query_grad * HEAD_DIM**-0.5)
        grads[1].append(jnp.concatenate(key_grads, axis=0))
        grads[2].append(jnp.concatenate(value_grads, axis=0))
    for place, pair in enumerate(grads):
        grad_ref[place] = jnp.where(low, pair[0], pair[1]).astype(BF)


def attend_back(qkv, attended, upstream, logs, first_rows, image_rows, start, deps=()):
    rows, wide = qkv.shape
    pairs, count = wide // 3 // LANES, attended.shape[1] // LANES
    part = lambda offset: pl.BlockSpec((rows, LANES), lambda i: (0, offset + i))
    return run(
        functools.partial(attend_back_kernel, first_rows, image_rows, 1),
        (qkv, qkv, qkv, attended, upstream, logs),
        shape_of((3, rows, count * LANES), BF),
        deps,
        [
            part(start),
            part(pairs + start),
            part(2 * pairs + start),
            part(0),
            part(start),
            pl.BlockSpec((1, 16, rows), lambda i: (i, 0, 0)),
        ],
        grid=(count,),
        out_specs=pl.BlockSpec((3, rows, LANES), lambda i: (0, 0, i)),
        name="attend_back",
        micros=5 * count,
    )


def qkv_grad_kernel(a_ref, *refs):
    turned = a_ref[...].T
    heads, out = refs[:-1], refs[-1]
    start = 0
    for kind in range(3):
        for part in heads:
            size = part.shape[2]
            out[:, start : start + size] = dot(turned, part[kind]).astype(BF)
            start += size


def qkv_grad(normed, heads, deps=()):
    width = normed.shape[1]
    return run(
        qkv_grad_kernel,
        (normed, *heads),
        shape_of((width, 3 * width), BF),
        deps,
        out_specs=INSIDE,
        name="qkv_grad",
        micros=6,
    )


def inputs_back_kernel(
    w_ref,
    x_ref,
    back_ref,
    table_ref,
    patch_ref,
    bilin_s_ref,
    bilin_l_ref,
    middle_rows_ref,
    b_one_ref,
    b_two_ref,
    *refs,
):
    heads, (large_ref, small_ref, woven, small_grad) = refs[:-4], refs[-4:]
    width = x_ref.shape[1]
    total, start = None, 0
    for kind in range(3):
        for part in heads:
            size = part.shape[2]
            value = dot(part[kind], w_ref[:, start : start + size], NT)
            total = value if total is None else total + value
            start += size
    first = POS_GRID * POS_GRID
    normal, inverse = norm_forward(x_ref[...])
    change, gain, shift = norm_backward(total, normal, inverse, table_ref[0][first + 1 : first + 2])
    grad = back_ref[...] + change
    low = grad.astype(BF)
    small = patch_ref.shape[0]
    large_ref[...] = low[small:]
    kern = dot(patch_ref[...], low[:small], TN)
    pixels = kern.shape[0] // 3
    for tile in range(width // LANES):
        woven[tile] = kern[:, tile * LANES : (tile + 1) * LANES]
        for channel in range(3):
            small_grad[
                channel * pixels : (channel + 1) * pixels, tile * LANES : (tile + 1) * LANES
            ] = woven[tile, pl.ds(channel, pixels, stride=3), :]
    table_grad_ref = small_grad.at[3 * pixels :]
    table_grad_ref[...] = jnp.zeros_like(table_grad_ref)
    tokens = bilin_l_ref.shape[0]
    large = grad[small : small + tokens]
    for image in range(1, (grad.shape[0] - small) // tokens):
        large = large + grad[small + image * tokens : small + (image + 1) * tokens]
    table_grad_ref[:first, :] = dot_fine(bilin_s_ref[...], grad[:small], TN) + dot_fine(
        bilin_l_ref[...], large, TN
    )
    table_grad_ref[first : first + 1, :] = jnp.sum(grad, axis=0, keepdims=True)
    table_grad_ref[first + 1 : first + 2, :] = gain
    table_grad_ref[first + 2 : first + 3, :] = shift
    table_grad_ref[first + 3 : first + 6, :] = middle_rows_ref[0:3, :]
    table_grad_ref[first + 6 : first + 7, :] = b_two_ref[...]
    for line in range(b_one_ref.shape[1] // width):
        table_grad_ref[first + 7 + line : first + 8 + line, :] = b_one_ref[
            :, line * width : (line + 1) * width
        ]
    rows = small_grad.shape[0]
    count = width // LANES // 2
    for tile in range(2 * count):
        side, level = divmod(tile, count)
        small_ref[level * rows : (level + 1) * rows, side * LANES : (side + 1) * LANES] = small_grad[
            :, tile * LANES : (tile + 1) * LANES
        ].astype(small_ref.dtype)


def inputs_back(
    heads, w_qkv, inputs, back, table_state, patches, bilin_s, bilin_l, rows_grads, bias_one, bias_two, kind
):
    rows, width = inputs.shape
    large = rows - patches.shape[0]
    operands = (
        w_qkv, inputs, back, table_state, patches, bilin_s, bilin_l, rows_grads, bias_one, bias_two, *heads
    )
    specs = [INSIDE] * len(operands)
    specs[3] = first_state(table_state)
    small = small_rows(patches.shape[1])
    return run(
        inputs_back_kernel,
        operands,
        [shape_of((large, width), BF), shape_of((small * width // LANES // 2, 2 * LANES), kind)],
        (),
        specs,
        grid=(1,),
        out_specs=[INSIDE] * 2,
        scratch_shapes=[
            pltpu.VMEM((width // LANES, patches.shape[1], LANES), F32),
            pltpu.VMEM((small, width), F32),
        ],
        name="inputs_back",
        micros=13,
    )


def small_rows(pixels):
    return -(-(pixels + TROWS) // 256) * 256


def base_back_kernel(projected_ref, large_ref, out_ref):
    width = large_ref.shape[1]
    large = large_ref[...]
    for channel in range(3):
        out_ref[:, channel * width : (channel + 1) * width] = dot(projected_ref[channel], large, TN)


def base_back(projected, large):
    rows, wide = projected.shape[2], 3 * large.shape[1]
    return run(
        base_back_kernel,
        (projected, large),
        shape_of((rows, wide), F32),
        out_specs=INSIDE,
        name="base_back",
        micros=8,
    )


def base_total_kernel(outer, where_ref, part_ref, small_ref, line_ref, out_ref, table_ref, squares_ref, sums):
    pixels = small_ref.shape[0]
    width = part_ref.shape[1] // 3
    count = width // LANES // 2
    height = sums.shape[1] * sums.shape[0] // line_ref.shape[0]
    rows = sums.shape[1] // count
    z, x, core, y = where_ref[0], where_ref[1], where_ref[2], where_ref[3]
    squares = jnp.zeros((1, LANES), F32)
    for place in range(line_ref.shape[0]):
        flip, pair, side, single = z ^ (place % outer), place // outer % 2, place // outer // 2 % 2, place // outer // 4
        block = flip * 4 + (x ^ pair) * 2 + (core ^ single)
        sums[y ^ side, pl.ds(pl.multiple_of(block * height, 8), height), :] = line_ref[place, :height]
    for block in range(line_ref.shape[0]):
        flip, pair, single, side = (block // 8) ^ z, (block // 4 % 2) ^ x, (block // 2 % 2) ^ core, (block % 2) ^ y
        squares = squares + line_ref[((single * 2 + side) * 2 + pair) * outer + flip, height : height + 1]
    squares_ref[1:2, :] = squares
    small = jnp.concatenate(
        [
            sums[tile // count, tile % count * rows : (tile % count + 1) * rows, :]
            for tile in range(2 * count)
        ],
        axis=1,
    )
    table_ref[...] = small[3 * pixels : 3 * pixels + table_ref.shape[0]]
    squares = jnp.zeros((1, LANES), F32)
    for channel in range(3):
        across = slice(channel * width, (channel + 1) * width)
        value = part_ref[:, across] + dot_fine(
            small_ref[...], small[channel * pixels : (channel + 1) * pixels], TN
        )
        out_ref[:, across] = value
        lines = jnp.sum(value * value, axis=0, keepdims=True)
        for start in range(0, width, LANES):
            squares = squares + lines[:, start : start + LANES]
    squares_ref[0:1, :] = squares


def base_total(place, part, resize_s, line, sums_rows):
    return run(
        functools.partial(base_total_kernel, place.outer),
        (place.where, part, resize_s, line),
        [shape_of(part.shape, F32), shape_of((TROWS, part.shape[1] // 3), F32), shape_of((2, LANES), F32)],
        (),
        [SCALARS] + [INSIDE] * 3,
        out_specs=[INSIDE] * 3,
        scratch_shapes=[pltpu.VMEM((2, sums_rows, LANES), F32)],
        name="base_total",
        micros=5,
    )


def adam_values(state, gradient, rate, scalars):
    clipped = gradient * scalars[0]
    first = BETA_ONE * state[1] + (1.0 - BETA_ONE) * clipped
    second = BETA_TWO * state[2] + (1.0 - BETA_TWO) * clipped * clipped
    movement = (first * scalars[1]) / (jnp.sqrt(second * scalars[2]) + ADAM_EPS)
    return state[0] - rate * (movement + DECAY * state[0]), first, second


def adam_kernel(count, scalars_ref, *refs):
    scalars = [scalars_ref[place] for place in range(3)]
    for place in range(count):
        state_ref, gradient_ref = refs[2 * place], refs[2 * place + 1]
        new_ref, moments_ref = refs[2 * count + 2 * place], refs[2 * count + 2 * place + 1]
        new, first, second = adam_values(
            state_ref[...], gradient_ref[...].astype(F32), scalars_ref[3 + place], scalars
        )
        new_ref[...] = new
        moments_ref[0] = first
        moments_ref[1] = second


def adam(scalars, states, gradients, steps):
    in_specs = [pl.BlockSpec(memory_space=pltpu.SMEM)]
    out_specs, out_shapes, operands = [], [], [scalars]
    for state, gradient in zip(states, gradients):
        rows, columns = state.shape[1:]
        part = rows // steps
        in_specs.append(pl.BlockSpec((3, part, columns), lambda i: (0, i, 0)))
        in_specs.append(pl.BlockSpec((part, columns), lambda i: (i, 0)))
        out_specs.append(pl.BlockSpec((part, columns), lambda i: (i, 0)))
        out_specs.append(pl.BlockSpec((2, part, columns), lambda i: (0, i, 0)))
        out_shapes.append(shape_of((rows, columns), F32))
        out_shapes.append(shape_of((2, rows, columns), F32))
        operands += [state, gradient]
    return pl.pallas_call(
        functools.partial(adam_kernel, len(states)),
        grid=(steps,),
        in_specs=in_specs,
        out_specs=out_specs,
        out_shape=out_shapes,
        compiler_params=params(),
        cost_estimate=cost(9e8, 0),
        name="optimizer",
    )(*operands)


class Place:
    def __init__(self):
        self.dp, self.mp = lax.axis_size("dp"), lax.axis_size("mp")
        self.index, self.column = lax.axis_index("dp"), lax.axis_index("mp")
        self.direct = self.mp == 2 and self.dp in (8, 16, 32, 64)
        self.outer = self.dp // 4
        self.z, self.x, self.core = self.index // 4, (self.index // 2) % 2, self.index % 2
        core = self.core if self.direct else jnp.zeros_like(self.core)
        self.where = jnp.stack([self.z, self.x, core, self.column]).astype(jnp.int32)

    def over_core(self, value):
        return lax.ppermute(value, "dp", [(i, i ^ 1) for i in range(self.dp)])

    def over_x(self, value):
        return lax.ppermute(value, "dp", [(i, i ^ 2) for i in range(self.dp)])

    def over_y(self, value):
        return lax.ppermute(value, "mp", [(0, 1), (1, 0)])

    def over_corner(self, value):
        return lax.ppermute(value, ("dp", "mp"), [(i, i ^ 5) for i in range(2 * self.dp)])

    def along_z(self, value, flip):
        return lax.ppermute(value, "dp", [(i, i ^ (4 * flip)) for i in range(self.dp)])


def pick(value, index, axis):
    return lax.dynamic_index_in_dim(value, index, axis, keepdims=False)


def assemble_kernel(outer, plan, where_ref, *refs):
    parts, wholes = refs[:8], refs[8:]
    height = parts[0].shape[1]
    z, x, core, y = where_ref[0], where_ref[1], where_ref[2], where_ref[3]
    for place, part in enumerate(parts):
        far_x, far_y, far_core = place & 1, (place >> 1) & 1, place >> 2
        column = y if far_y == 0 else 1 - y
        pair = x if far_x == 0 else 1 - x
        single = core if far_core == 0 else 1 - core
        for slot in range(outer):
            block = (z ^ slot) * 4 + pair * 2 + single
            for array, start, width, rows, offset in plan:
                wholes[array][
                    pl.ds(pl.multiple_of(block * rows + offset, 16), height),
                    pl.ds(pl.multiple_of(column * width, LANES), width),
                ] = part[slot, :, start : start + width]


def assemble(place, parts, plan, deps=()):
    outer, height = parts[0].shape[:2]
    sizes = {array: (place.dp * rows, 2 * width) for array, _, width, rows, _ in plan}
    return run(
        functools.partial(assemble_kernel, outer, plan),
        (place.where, *parts),
        [shape_of(sizes[array], BF) for array in sorted(sizes)],
        deps,
        [SCALARS] + [INSIDE] * 8,
        out_specs=[INSIDE] * len(sizes),
        name="assemble",
        micros=4,
    )


def assemble_rows_kernel(outer, where_ref, line_ref, out):
    height = line_ref.shape[1]
    z, x, core, y = where_ref[0], where_ref[1], where_ref[2], where_ref[3]
    for place in range(line_ref.shape[0]):
        flip, rest = place % outer, place // outer
        block = (z ^ flip) * 4 + (x ^ (rest & 1)) * 2 + (core ^ (rest >> 2))
        row = pl.multiple_of((block * 2 + (y ^ ((rest >> 1) & 1))) * height, 16)
        out[pl.ds(row, height), :] = line_ref[place]


def assemble_rows(place, line):
    count, height, width = line.shape
    return run(
        functools.partial(assemble_rows_kernel, place.outer),
        (place.where, line),
        shape_of((count * height, width), BF),
        (),
        [SCALARS, INSIDE],
        out_specs=INSIDE,
        name="assemble",
        micros=2,
    )


def behind(value, after):
    return lax.optimization_barrier((value, after))[0]


class Gather:
    def __init__(self, place, own):
        self.place = place
        self.first = [own] + [place.along_z(own, flip) for flip in range(1, place.outer)]

    def sides(self, after=()):
        place = self.place
        self.line = jnp.stack(behind(self.first, after))
        self.by_x, self.by_y = place.over_x(self.line), place.over_y(self.line)

    def corner(self, after=()):
        place, half = self.place, self.place.outer // 2
        by_x, by_y = behind((self.by_x, self.by_y), after)
        self.far = (place.over_y(by_x[:half]), place.over_x(by_y[half:]))
        near = [self.line, self.by_x, self.by_y, jnp.concatenate(self.far, axis=0)]
        self.parts = near + [place.over_core(part) for part in near]


def add_low(left, right):
    return left + right


def first_sum_kernel(plan, where_ref, *refs):
    count = len(plan)
    keeps, comes, outs = refs[:count], refs[count : 2 * count], refs[2 * count :]
    x, core, y = where_ref[1], where_ref[2], where_ref[3]
    height = outs[0].shape[2]
    half = keeps[0].shape[0] // 4
    for keep, come, (width, start) in zip(keeps, comes, plan):
        for piece in range(keep.shape[2] // height):
            down = slice(piece * height, (piece + 1) * height)
            into = slice(start + piece * width, start + (piece + 1) * width)
            for column in range(2):
                across = slice(column * width, (column + 1) * width)
                for level in range(half):
                    for out, value in ((outs[0], x), (outs[1], 1 - x)):
                        at = 2 * level + value
                        out[column, level, :, into] = add_low(
                            keep[at, core, down, across], come[at, down, across]
                        )
            for place in range(2 * half):
                at = 2 * half + place
                for out, value in ((outs[2], y), (outs[3], 1 - y)):
                    across = pl.ds(pl.multiple_of(value * width, LANES), width)
                    out[place, :, into] = add_low(keep[at, core, down, across], come[at, down, across])


def second_sum_kernel(where_ref, *refs):
    x, y = where_ref[1], where_ref[3]
    keep, come, keep_low, come_low, *outs = refs
    for level in range(keep.shape[1]):
        for out, value in ((outs[0], y), (outs[1], 1 - y)):
            out[level] = add_low(keep[value, level], come[value, level])
    for level in range(keep_low.shape[0] // 2):
        for out, value in ((outs[2], x), (outs[3], 1 - x)):
            at = 2 * level + value
            out[level] = add_low(keep_low[at], come_low[at])


def third_sum_kernel(where_ref, *refs):
    line = refs[-1]
    z, outer = where_ref[0], line.shape[0]
    operands, outs = refs[: -1 - outer], refs[-1 - outer : -1]
    start = 0
    for keep, come in zip(operands[0::2], operands[1::2]):
        for level in range(keep.shape[0]):
            line[start + level] = add_low(keep[level], come[level])
        start += keep.shape[0]
    for shift, out in enumerate(outs):
        out[...] = line[z ^ shift]


def last_sum_kernel(wide, more, *refs):
    parts, outs = refs[: len(refs) - 2 - more], refs[len(refs) - 2 - more :]
    total_ref, share_ref = outs[-2:]
    total = parts[0][...].astype(F32)
    for part in parts[1:]:
        total = total + part[...].astype(F32)
    total_ref[...] = total[:, :wide]
    lines = jnp.sum(total[:, :wide] * total[:, :wide], axis=0, keepdims=True)
    squares = lines[:, :LANES]
    for start in range(LANES, wide, LANES):
        squares = squares + lines[:, start : start + LANES]
    if more:
        height = total.shape[0]
        share_ref[:height, :] = total[:, wide:]
        share_ref[height:, :] = jnp.zeros((8, LANES), F32)
        share_ref[height : height + 1, :] = squares + outs[0][...]
    else:
        share_ref[...] = squares


class Scatter:
    def __init__(self, place, grads, height, deps=()):
        self.place = place
        half = place.outer // 2
        keeps = [g.reshape(2 * place.outer, 2, g.shape[0] // place.dp, g.shape[1]) for g in grads]
        comes = [place.over_core(pick(keep, 1 - place.core, 1)) for keep in keeps]
        plan, total = [], 0
        for keep in keeps:
            plan.append((keep.shape[3] // 2, total))
            total += keep.shape[2] // height * keep.shape[3] // 2
        shapes = [shape_of((2, half, height, total), BF)] * 2
        shapes += [shape_of((2 * half, height, total), BF)] * 2
        self.first = self.call(functools.partial(first_sum_kernel, plan), (*keeps, *comes), shapes, deps)
        self.came_first = (place.over_x(self.first[1]), place.over_y(self.first[3]))
        self.size = (height, total)

    def call(self, kernel, operands, shapes, deps=(), name="sum", **rest):
        return run(
            kernel,
            (self.place.where, *operands),
            shapes,
            deps,
            [SCALARS] + [INSIDE] * len(operands),
            out_specs=[INSIDE] * len(shapes),
            name=name,
            micros=2,
            **rest,
        )

    def second(self, deps=()):
        place = self.place
        operands = [v for pair in zip(self.first[0::2], self.came_first) for v in pair]
        shapes = [shape_of((place.outer // 2,) + self.size, BF)] * 4
        self.next = self.call(second_sum_kernel, operands, shapes, deps)
        self.came_second = (place.over_y(self.next[1]), place.over_x(self.next[3]))
        return self.next[1::2]

    def third(self, deps=()):
        place, outer = self.place, self.place.outer
        operands = [v for pair in zip(self.next[0::2], self.came_second) for v in pair]
        lines = self.call(
            third_sum_kernel,
            operands,
            [shape_of(self.size, BF)] * outer,
            deps,
            scratch_shapes=[pltpu.VMEM((outer,) + self.size, BF)],
        )
        self.sent = lines[1:]
        self.lines = [lines[0]] + [
            place.along_z(line, shift) for shift, line in enumerate(lines[1:], start=1)
        ]
        return self.lines

    def last(self, squares=None, deps=()):
        height, wide = self.size
        if squares is None:
            share, more = shape_of((1, LANES), F32), ()
        else:
            wide -= LANES
            share, more = shape_of((height + 8, LANES), F32), (squares,)
        return run(
            functools.partial(last_sum_kernel, wide, len(more)),
            tuple(self.lines) + more,
            [shape_of((height, wide), F32), share],
            deps,
            out_specs=[INSIDE] * 2,
            name="total",
            micros=1,
        )


def spread_share(place, share, after_line=(), after_near=()):
    line = [share] + [place.along_z(share, flip) for flip in range(1, place.outer)]
    line = jnp.stack(behind(line, after_line))
    near = [line, place.over_x(line), place.over_y(line), place.over_corner(line)]
    near = jnp.concatenate(behind(near, after_near), axis=0)
    return jnp.concatenate([near, place.over_core(near)], axis=0)


def scatter_plain(grad):
    rows = lax.psum_scatter(grad, "dp", scatter_dimension=0, tiled=True)
    return lax.psum_scatter(rows, "mp", scatter_dimension=1, tiled=True).astype(F32)


def gather_plain(shard):
    rows = lax.all_gather(shard.astype(BF), "dp", axis=0, tiled=True)
    return lax.all_gather(rows, "mp", axis=1, tiled=True)


def body(
    kernel_state,
    qkv_state,
    proj_state,
    fc1_state,
    fc2_state,
    table_state,
    patches_s,
    patches_l,
    resize_s,
    resize_l,
    bilin_s,
    bilin_l,
    cotangent,
    rates,
    step,
):
    place = Place()
    where, direct = place.where, place.direct
    first = POS_GRID * POS_GRID
    bias_one = table_state[0, first + 7 :].reshape(1, -1)
    low = lambda state: state[0].astype(BF)
    height, wide = qkv_state.shape[1:]
    hidden = fc1_state.shape[2]
    units = fc2_state.shape[1]
    side = proj_state.shape[2]
    if direct:
        pieces = units // height
        first_gather = Gather(place, low(qkv_state))
        first_gather.sides()
        shard = [low(fc1_state)] + list(low(fc2_state).reshape(pieces, height, side)) + [low(proj_state)]
        second_gather = Gather(place, jnp.concatenate(shard, axis=1))
        plan = [(0, 0, hidden, height, 0)]
        plan += [(1, hidden + piece * side, side, units, piece * height) for piece in range(pieces)]
        plan += [(2, hidden + pieces * side, side, height, 0)]

    images, image_rows = patches_l.shape[0], patches_l.shape[1]
    large_rows = images * image_rows // place.mp
    projected, embed_part, kern_part = resize_forward(
        kernel_state, resize_s, resize_l, patches_l.reshape(images * image_rows, -1)
    )
    if direct:
        kern = kern_part + place.over_y(kern_part.astype(BF)).astype(F32)
        parts = embed_part.reshape(place.mp, large_rows, -1)
        embed_large = pick(parts, place.column, 0) + place.over_y(pick(parts, 1 - place.column, 0))
    else:
        kern = lax.psum(kern_part, "mp")
        embed_large = lax.psum_scatter(embed_part, "mp", scatter_dimension=0, tiled=True)
    patches_own = pick(patches_s, place.column, 0)
    first_rows = patches_own.shape[0]
    inputs, normed_one = embed(patches_own, kern, embed_large, bilin_s, bilin_l, table_state)

    if direct:
        first_gather.corner((normed_one, second_gather.first))
        second_gather.sides(first_gather.far)
        (w_qkv,) = assemble(place, first_gather.parts, [(0, 0, wide, height, 0)])
    else:
        w_qkv = gather_plain(qkv_state[0])
    qkv_rows = product(normed_one, w_qkv, D)
    pairs = D // LANES // 2
    attention = []
    for call in range(2):
        waits = (second_gather.line,) if direct and call == 0 else ()
        attention.append(attend(qkv_rows, first_rows, image_rows, call * pairs, pairs, waits))
    attended = [call[0] for call in attention]

    if direct:
        second_gather.corner(attended)
        w_fc1, w_fc2, w_proj = assemble(place, second_gather.parts, plan)
    else:
        w_proj, w_fc1, w_fc2 = [gather_plain(a[0]) for a in (proj_state, fc1_state, fc2_state)]
    middle, normed_two = merge(inputs, attended, w_proj, table_state)
    block_out, back, grad_fc1, grad_fc2, bias_one_grad, bias_two_grad = feed(
        middle, cotangent, normed_two, w_fc1, w_fc2, bias_one, table_state
    )
    middle_grad, heads_up, middle_rows, grad_proj = merge_back(
        back, middle, cotangent, attended, w_proj, table_state
    )
    waits = ()
    if direct:
        scatter_f = Scatter(place, (grad_fc1, grad_fc2, grad_proj), height)
        waits = tuple(scatter_f.first[1::2])
    heads = [
        attend_back(
            qkv_rows, attended[call], heads_up, attention[call][1], first_rows, image_rows,
            call * pairs, waits,
        )
        for call in range(2)
    ]
    large_grad, small_grad = inputs_back(
        heads,
        w_qkv,
        inputs,
        middle_grad,
        table_state,
        patches_own,
        bilin_s,
        bilin_l,
        middle_rows,
        bias_one_grad,
        bias_two_grad,
        BF if direct else F32,
    )
    waits = tuple(scatter_f.second()) if direct else ()
    grad_qkv = qkv_grad(normed_one, heads, waits)
    kern_rows = patches_s.shape[2]
    if direct:
        projected = behind(projected, second_gather.far)
        projected = lax.all_gather(projected, "dp", axis=1, tiled=True)
        scatter_f.third()
        scatter_q = Scatter(place, (grad_qkv, small_grad), height, tuple(scatter_f.sent))
        scatter_q.second()
        large_all = assemble_rows(
            place, spread_share(place, large_grad, scatter_q.first[1::2], scatter_q.next[1::2])
        )
        scatter_q.third()
        own_rest, squares_f = scatter_f.last(None, tuple(scatter_q.sent))
        part = base_back(projected, large_all)
        own_qkv, share = scatter_q.last(squares_f, (part,))
        base_grad, table_total, squares = base_total(
            place, part, resize_s, spread_share(place, share), small_grad.shape[0]
        )
        own_fc2 = jnp.concatenate(
            [own_rest[:, hidden + piece * side : hidden + (piece + 1) * side] for piece in range(pieces)],
            axis=0,
        )
        owned = (own_qkv, own_rest[:, hidden + pieces * side :], own_rest[:, :hidden], own_fc2)
        square_total = jnp.sum(squares[1] + (squares[0] + place.over_y(squares[:1])[0]))
    else:
        large_all = lax.all_gather(large_grad, "mp", axis=0, tiled=True)
        sums = lax.psum(small_grad, ("dp", "mp"))
        sums = sums.reshape(D // LANES // 2, -1, 2, LANES).transpose(1, 2, 0, 3).reshape(-1, D)
        table_total = sums[kern_rows : kern_rows + TROWS]
        part = lax.dot_general(
            resize_s,
            sums[:kern_rows].reshape(3, -1, D).transpose(1, 0, 2).reshape(-1, 3 * D),
            TN,
            precision=lax.Precision.HIGHEST,
            preferred_element_type=F32,
        )
        base_grad = lax.psum(base_back(projected, large_all), "dp") + part
        owned = tuple(scatter_plain(g) for g in (grad_qkv, grad_proj, grad_fc1, grad_fc2))
        squares = sum(jnp.sum(piece * piece) for piece in owned)
        square_total = lax.psum(squares, ("dp", "mp")) + lax.psum(
            jnp.sum(base_grad * base_grad), "mp"
        )
    grad_norm = jnp.sqrt(square_total + jnp.sum(table_total * table_total))
    clip_level = 0.5 * math.sqrt(3 * BASE * BASE * D + 4 * D * D + 2 * D * FF + TROWS * D)
    factor = clip_level / jnp.maximum(grad_norm, clip_level)
    count = step[0].astype(F32)
    fix_one = 1.0 / (1.0 - jnp.power(BETA_ONE, count))
    fix_two = 1.0 / (1.0 - jnp.power(BETA_TWO, count))
    fixed = jnp.stack([factor, fix_one, fix_two])
    blocks = adam(
        jnp.concatenate([fixed, rates[1:]]),
        (qkv_state, proj_state, fc1_state, fc2_state, table_state),
        owned + (table_total,),
        1,
    )
    kernel_new, kernel_moments = adam(
        jnp.concatenate([fixed, rates[:1]]), (kernel_state,), (base_grad,), kernel_state.shape[1] // 64
    )
    return (block_out, grad_norm, kernel_new, kernel_moments, *blocks)


def solution(mesh):
    placed = (
        P(None, "mp", None),
        P(None, "dp", "mp"),
        P(None, "dp", "mp"),
        P(None, "dp", "mp"),
        P(None, "dp", "mp"),
        P(),
        P("dp", None, None),
        P("dp", None, None),
        P(None, "mp"),
        P(None, "mp"),
        P(),
        P(),
        P(("dp", "mp"), None),
        P(),
        P(),
    )
    return jax.shard_map(
        body,
        mesh=mesh,
        in_specs=placed,
        out_specs=(
            P(("dp", "mp"), None),
            P(),
            P("mp", None),
            P(None, "mp", None),
            P("dp", "mp"),
            P(None, "dp", "mp"),
            P("dp", "mp"),
            P(None, "dp", "mp"),
            P("dp", "mp"),
            P(None, "dp", "mp"),
            P("dp", "mp"),
            P(None, "dp", "mp"),
            P(),
            P(),
        ),
        check_vma=False,
    )
```

time: 503 us -> 448 us (0.89)
  waiting for transfers between devices: 166 us -> 81.1 us
  Pallas kernels: 172 us -> 222 us
  starting transfers between devices: 87.5 us -> 69 us
  other arithmetic: 28.3 us -> 12.5 us
  between operations: 8.65 us -> 18.2 us
    pallas_call x11 -> x23, Pallas kernels: 138 us -> 187 us  [run(): pl.pallas_call(inner, in_specs=list(in_specs) + [pl.BlockSpec(memory_spac...]
    ppermute x20 -> x13, waiting for transfers between devices: 73 us -> 24.3 us  [over_y(): return lax.ppermute(value, 'mp', [(0, 1), (1, 0)])]
    ppermute x18 -> x10, waiting for transfers between devices: 46.6 us -> 19.9 us  [over_x(): return lax.ppermute(value, 'dp', [(i, i ^ 2) for i in range(self.dp)])]
    ppermute x31 -> x20, waiting for transfers between devices: 46 us -> 30.2 us  [the longest x18 28.3 us: along_z(): lax.ppermute(value, 'dp', [(i, i ^ 4 * flip) for i in range(self.dp)])]
    ppermute x20 -> x13, starting transfers between devices: 24.7 us -> 14.7 us  [over_y(): return lax.ppermute(value, 'mp', [(0, 1), (1, 0)])]
    convert_element_type x22 -> x0, other arithmetic: 8.71 us -> none  [add_low(): return (left.astype(F32) + right.astype(F32)).astype(BF)]
    squeeze x11 -> x6, local copies, waits for them, and re-layouts: 2.08 us -> 9.68 us  [pick(): return lax.dynamic_index_in_dim(value, index, axis, keepdims=False)]
    dynamic_slice x12 -> x2, local copies, waits for them, and re-layouts: 8.5 us -> 0.99 us  [pick(): return lax.dynamic_index_in_dim(value, index, axis, keepdims=False)]
  transfers between devices with their start and end apart: 89 -> 59, of which waited for: 33 -> 25; matrix products, arithmetic and copies ran while one was open for 11% -> 6% of each run, Pallas kernels for 12% -> 33%
where the time goes in v2:
time: 448 us; the launch traced here: 439 us
  Pallas kernels  222 us (50%)
  waiting for transfers between devices  81.1 us (18%)
  starting transfers between devices  69 us (15%)
  local copies, waits for them, and re-layouts  36.5 us (8%)
  between operations  18.2 us (4%)
  other arithmetic  12.5 us (3%)
    pallas_call x23, Pallas kernels, run(): pl.pallas_call(inner, in_specs=list(in_specs) + [pl.BlockSpec(memory_spac...  187 us
    ppermute x18, starting transfers between devices, along_z(): lax.ppermute(value, 'dp', [(i, i ^ 4 * flip) for i in range(self.dp)])  38.8 us
    ppermute x18, waiting for transfers between devices, along_z(): lax.ppermute(value, 'dp', [(i, i ^ 4 * flip) for i in range(self.dp)])  28.3 us
    ppermute x13, waiting for transfers between devices, over_y(): return lax.ppermute(value, 'mp', [(0, 1), (1, 0)])  24.3 us
    ppermute x10, waiting for transfers between devices, over_x(): return lax.ppermute(value, 'dp', [(i, i ^ 2) for i in range(self.dp)])  19.9 us
    unnamed x105, local copies, waits for them, and re-layouts  19 us
    pallas_call x2, Pallas kernels, adam(): pl.pallas_call(functools.partial(adam_kernel, len(states)), grid=(steps,)...  18.6 us
    ppermute x13, starting transfers between devices, over_y(): return lax.ppermute(value, 'mp', [(0, 1), (1, 0)])  14.7 us
  transfers between devices with their start and end apart: 59, of which 25 were waited for; matrix products, arithmetic and copies ran while one was open for 6% of the time, Pallas kernels for 33%

profile of v2, /device:TPU:0, one launch (start us, length us, event | category | flops | bytes accessed | tf_op | source)
XLA Modules:
  0.0 439.4 jit_solution(18061209984327486779)
XLA Ops:
  13.9 9.5 %resize.1 = (bf16[3,64,512]{2,1,0:T(8,128)(2,1)}, f32[64,768]{1,0:T(8,128)}, f32[64,2304]{1,0:T(8,128)}) custom-call(f32[3,512,2304]{2,1,0:T(8,128)} %refs_0_.2, f32[64,512]{1,0:T(8,128)} %refs_2_.6, f32[2304,512]{1,0:T(8,128)} %large_ref.1, bf16[64,6912]{1,0:T(8,128)(2,1)} %bitcast.85), custom_call_target="tpu_custom_call" | custom-call | flops 900000000 | tf_op jit(solution)/shard_map/resize/pallas_call | solution.py:158
  42.5 5.0 %embed.1 = (f32[816,768]{1,0:T(8,128)}, bf16[816,768]{1,0:T(8,128)(2,1)}) custom-call(bf16[784,192]{1,0:T(8,128)(2,1)} %bitcast.79, f32[64,2304]{1,0:T(8,128)} %convert_add_fusion.refs_1_, f32[32,768]{1,0:T(8,128)} %bitcast_add_fusion.refs_2_, f32[784,49]{1,0:T(8,128)} %copy.30.refs_3_.refs_5_, f32[16,49]{1,0:T(8,128)} %refs_6_.4, f32[3,60,768]{2,1,0:T(8,128)} %refs_8_.1), custom_call_target="tpu_custom_call" | custom-call | flops 500000000 | tf_op jit(solution)/shard_map/embed/pallas_call | solution.py:62
  47.5 12.7 %collective-permute-done.3 = bf16[48,3456]{1,0:T(8,128)(2,1)S(1)} collective-permute-done((bf16[48,3456]{1,0:T(8,128)(2,1)S(1)}, bf16[48,3456]{1,0:T(8,128)(2,1)S(1)}, u32[]{:S(2)}, u32[]{:S(2)}) %collective-permute-start.3) | collective-permute-done | bytes 331808 | tf_op jit(solution)/shard_map/ppermute | solution.py:773
  66.3 4.9 %collective-permute-done.11 = bf16[2,48,1152]{2,1,0:T(8,128)(2,1)S(1)} collective-permute-done((bf16[2,48,1152]{2,1,0:T(8,128)(2,1)S(1)}, bf16[2,48,1152]{2,1,0:T(8,128)(2,1)S(1)}, u32[]{:S(2)}, u32[]{:S(2)}) %collective-permute-start.11) | collective-permute-done | bytes 221216 | tf_op jit(solution)/shard_map/ppermute | solution.py:764
  84.0 6.8 %project.1.refs_0_.refs_1_.refs_2_ = bf16[816,2304]{1,0:T(8,128)(2,1)} custom-call(bf16[816,768]{1,0:T(8,128)(2,1)} %get-tuple-element.119.left_ref.refs_0_, bf16[768,2304]{1,0:T(8,128)(2,1)} %assemble.3.right_ref.refs_0_), custom_call_target="tpu_custom_call" | custom-call | flops 700000000 | tf_op jit(solution)/shard_map/project/pallas_call | solution.py:239
  90.8 10.1 %attend.2 = (bf16[816,384]{1,0:T(8,128)(2,1)}, f32[3,16,816]{2,1,0:T(8,128)}) custom-call(bf16[816,2304]{1,0:T(8,128)(2,1)} %project.1.refs_0_.refs_1_.refs_2_, bf16[816,2304]{1,0:T(8,128)(2,1)} %project.1.refs_0_.refs_1_.refs_2_, bf16[816,2304]{1,0:T(8,128)(2,1)} %project.1.refs_0_.refs_1_.refs_2_, bf16[4,48,3456]{2,1,0:T(8,128)(2,1)} %pad_maximum_fusion.refs_3_.refs_1_), custom_call_target="tpu_custom_call" | custom-call | flops 900000000 | tf_op jit(solution)/shard_map/attend/pallas_call | solution.py:62
  100.9 10.4 %attend.3 = (bf16[816,384]{1,0:T(8,128)(2,1)}, f32[3,16,816]{2,1,0:T(8,128)}) custom-call(bf16[816,2304]{1,0:T(8,128)(2,1)} %project.1.refs_0_.refs_1_.refs_2_, bf16[816,2304]{1,0:T(8,128)(2,1)} %project.1.refs_0_.refs_1_.refs_2_, bf16[816,2304]{1,0:T(8,128)(2,1)} %project.1.refs_0_.refs_1_.refs_2_), custom_call_target="tpu_custom_call" | custom-call | flops 900000000 | tf_op jit(solution)/shard_map/attend/pallas_call | solution.py:62
  114.2 14.5 %collective-permute-done.18 = bf16[2,48,3456]{2,1,0:T(8,128)(2,1)S(1)} collective-permute-done((bf16[2,48,3456]{2,1,0:T(8,128)(2,1)S(1)}, bf16[2,48,3456]{2,1,0:T(8,128)(2,1)S(1)}, u32[]{:S(2)}, u32[]{:S(2)}) %collective-permute-start.18) | collective-permute-done | bytes 663584 | tf_op jit(solution)/shard_map/ppermute | solution.py:767
  134.4 9.0 %assemble.4 = (bf16[768,3072]{1,0:T(8,128)(2,1)}, bf16[3072,768]{1,0:T(8,128)(2,1)}, bf16[768,768]{1,0:T(8,128)(2,1)}) custom-call(s32[4]{0:T(128)} %pad_add_fusion.refs_0_, bf16[4,48,3456]{2,1,0:T(8,128)(2,1)} %pad_maximum_fusion.refs_3_.refs_1_, bf16[4,48,3456]{2,1,0:T(8,128)(2,1)} %copy-done.4, bf16[4,48,3456]{2,1,0:T(8,128)(2,1)} %copy-done.5, ...), custom_call_target="tpu_custom_call" | custom-call | flops 400000000 | tf_op jit(solution)/shard_map/assemble/pallas_call | solution.py:62
  143.4 6.1 %merge.1 = (f32[816,768]{1,0:T(8,128)}, bf16[816,768]{1,0:T(8,128)(2,1)}) custom-call(f32[816,768]{1,0:T(8,128)} %get-tuple-element.114.refs_0_.refs_1_, bf16[768,768]{1,0:T(8,128)(2,1)} %get-tuple-element.130.refs_1_.refs_3_, f32[3,60,768]{2,1,0:T(8,128)} %refs_8_.1, bf16[816,384]{1,0:T(8,128)(2,1)} %get-tuple-element.126.refs_3_.refs_5_, ...), custom_call_target="tpu_custom_call" | custom-call | flops 600000000 | tf_op jit(solution)/shard_map/merge/pallas_call | solution.py:62
  149.4 33.4 %feed.1 = (f32[816,768]{1,0:T(8,128)}, f32[816,768]{1,0:T(8,128)}, bf16[768,3072]{1,0:T(8,128)(2,1)}, bf16[3072,768]{1,0:T(8,128)(2,1)}, f32[1,3072]{1,0:T(1,128)}, /*index=5*/f32[1,768]{1,0:T(1,128)}) custom-call(f32[816,768]{1,0:T(8,128)} %get-tuple-element.131.refs_0_.refs_1_, f32[816,768]{1,0:T(8,128)} %refs_2_.5, ...), custom_call_target="tpu_custom_call" | custom-call | flops 3600000000 | tf_op jit(solution)/shard_map/feed/pallas_call | solution.py:62
  188.4 8.8 %merge_back.1 = (f32[816,768]{1,0:T(8,128)}, bf16[816,768]{1,0:T(8,128)(2,1)}, f32[8,768]{1,0:T(8,128)}, bf16[768,768]{1,0:T(8,128)(2,1)}) custom-call(f32[816,768]{1,0:T(8,128)} %get-tuple-element.138.refs_0_, f32[816,768]{1,0:T(8,128)} %get-tuple-element.131.refs_0_.refs_1_, f32[816,768]{1,0:T(8,128)} %refs_2_.5, ...), custom_call_target="tpu_custom_call" | custom-call | flops 900000000 | tf_op jit(solution)/shard_map/merge_back/pallas_call | solution.py:62
  201.9 8.6 %sum.6 = (bf16[2,2,48,3456]{3,2,1,0:T(8,128)(2,1)}, bf16[2,2,48,3456]{3,2,1,0:T(8,128)(2,1)}, bf16[4,48,3456]{2,1,0:T(8,128)(2,1)}, bf16[4,48,3456]{2,1,0:T(8,128)(2,1)}) custom-call(s32[4]{0:T(128)} %pad_add_fusion.refs_0_, bf16[8,2,48,3072]{3,2,1,0:T(8,128)(2,1)} %bitcast.76, bf16[8,2,192,768]{3,2,1,0:T(8,128)(2,1)} %bitcast.77, ...), custom_call_target="tpu_custom_call" | custom-call | flops 200000000 | tf_op jit(solution)/shard_map/sum/pallas_call | solution.py:62
  212.1 16.1 %attend_back.3.refs_11_.refs_2_ = bf16[3,816,384]{2,1,0:T(8,128)(2,1)} custom-call(bf16[816,2304]{1,0:T(8,128)(2,1)} %project.1.refs_0_.refs_1_.refs_2_, bf16[816,2304]{1,0:T(8,128)(2,1)} %project.1.refs_0_.refs_1_.refs_2_, bf16[816,2304]{1,0:T(8,128)(2,1)} %project.1.refs_0_.refs_1_.refs_2_, bf16[816,384]{1,0:T(8,128)(2,1)} %get-tuple-element.127.refs_4_.refs_6_.refs_3_, ...), custom_call_target="tpu_custom_call" | custom-call | flops 1500000000 | tf_op jit(solution)/shard_map/attend_back/pallas_call | solution.py:62
  228.2 16.1 %attend_back.2.refs_10_.refs_1_ = bf16[3,816,384]{2,1,0:T(8,128)(2,1)} custom-call(bf16[816,2304]{1,0:T(8,128)(2,1)} %project.1.refs_0_.refs_1_.refs_2_, bf16[816,2304]{1,0:T(8,128)(2,1)} %project.1.refs_0_.refs_1_.refs_2_, bf16[816,2304]{1,0:T(8,128)(2,1)} %project.1.refs_0_.refs_1_.refs_2_, bf16[816,384]{1,0:T(8,128)(2,1)} %get-tuple-element.126.refs_3_.refs_5_, ...), custom_call_target="tpu_custom_call" | custom-call | flops 1500000000 | tf_op jit(solution)/shard_map/attend_back/pallas_call | solution.py:62
  244.4 6.0 %collective-permute-done.30.refs_2_ = bf16[2,2,48,3456]{3,2,1,0:T(8,128)(2,1)S(1)} collective-permute-done((bf16[2,2,48,3456]{3,2,1,0:T(8,128)(2,1)}, bf16[2,2,48,3456]{3,2,1,0:T(8,128)(2,1)S(1)}, u32[]{:S(2)}, u32[]{:S(2)}) %collective-permute-start.30) | collective-permute-done | bytes 1327136 | tf_op jit(solution)/shard_map/ppermute | solution.py:764
  256.1 9.0 %qkv_grad.1 = bf16[768,2304]{1,0:T(8,128)(2,1)} custom-call(bf16[816,768]{1,0:T(8,128)(2,1)} %get-tuple-element.119.left_ref.refs_0_, bf16[3,816,384]{2,1,0:T(8,128)(2,1)} %attend_back.2.refs_10_.refs_1_, bf16[3,816,384]{2,1,0:T(8,128)(2,1)} %attend_back.3.refs_11_.refs_2_, bf16[2,48,3456]{2,1,0:T(8,128)(2,1)} %get-tuple-element.154.refs_3_, ...), custom_call_target="tpu_custom_call" | custom-call | flops 600000000 | tf_op jit(solution)/shard_map/qkv_grad/pallas_call | solution.py:62
  268.6 13.4 %inputs_back.1 = (bf16[32,768]{1,0:T(8,128)(2,1)}, bf16[768,256]{1,0:T(8,128)(2,1)}) custom-call(bf16[768,2304]{1,0:T(8,128)(2,1)} %assemble.3.right_ref.refs_0_, f32[816,768]{1,0:T(8,128)} %get-tuple-element.114.refs_0_.refs_1_, f32[816,768]{1,0:T(8,128)} %get-tuple-element.139.refs_2_, f32[3,60,768]{2,1,0:T(8,128)} %refs_8_.1, bf16[784,192]{1,0:T(8,128)(2,1)} %bitcast.80, ...), custom_call_target="tpu_custom_call" | custom-call | flops 1300000000 | tf_op jit(solution)/shard_map/inputs_back/pallas_call | solution.py:62
  326.1 6.5 %collective-permute-done.43.refs_4_ = bf16[2,48,1280]{2,1,0:T(8,128)(2,1)S(1)} collective-permute-done((bf16[2,48,1280]{2,1,0:T(8,128)(2,1)S(1)}, bf16[2,48,1280]{2,1,0:T(8,128)(2,1)S(1)}, u32[]{:S(2)}, u32[]{:S(2)}) %collective-permute-start.43) | collective-permute-done | bytes 245792 | tf_op jit(solution)/shard_map/ppermute | solution.py:764
  339.0 8.0 %collective-permute-done.48.refs_2_ = bf16[48,3456]{1,0:T(8,128)(2,1)S(1)} collective-permute-done((bf16[48,3456]{1,0:T(8,128)(2,1)S(1)}, bf16[48,3456]{1,0:T(8,128)(2,1)S(1)}, u32[]{:S(2)}, u32[]{:S(2)}) %collective-permute-start.48) | collective-permute-done | bytes 331808 | tf_op jit(solution)/shard_map/ppermute | solution.py:773
  356.7 7.2 %base_back.1.refs_5_.refs_1_ = f32[512,2304]{1,0:T(8,128)} custom-call(bf16[3,1024,512]{2,1,0:T(8,128)(2,1)} %all-gather.2.cloned.1.call-done.refs_0_, bf16[1024,768]{1,0:T(8,128)(2,1)} %assemble.5.refs_1_), custom_call_target="tpu_custom_call" | custom-call | flops 800000000 | tf_op jit(solution)/shard_map/base_back/pallas_call | solution.py:62
  366.6 10.2 %collective-permute-start.50 = (f32[56,128]{1,0:T(8,128)}, f32[56,128]{1,0:T(8,128)S(1)}, u32[]{:S(2)}, u32[]{:S(2)}) collective-permute-start(f32[56,128]{1,0:T(8,128)} %get-tuple-element.185), channel_id=1, source_target_pairs={{0,8},{2,10},{4,12},{6,14},{8,0},{10,2},{12,4},{14,6},{16,24},{18,... | collective-permute-start | bytes 86024 | tf_op jit(solution)/shard_map/ppermute | solution.py:773
  395.1 7.0 %base_total.1 = (f32[512,2304]{1,0:T(8,128)}, f32[60,768]{1,0:T(8,128)}, f32[2,128]{1,0:T(2,128)}) custom-call(s32[4]{0:T(128)} %pad_add_fusion.refs_0_, f32[512,2304]{1,0:T(8,128)} %base_back.1.refs_5_.refs_1_, f32[64,512]{1,0:T(8,128)} %refs_2_.6, f32[32,56,128]{2,1,0:T(8,128)} %copy-done.13), custom_call_target="tpu_custom_call" | custom-call | flops 500000000 | tf_op jit(solution)/shard_map/base_total/pallas_call | solution.py:62
  416.4 14.5 %optimizer.2 = (f32[512,2304]{1,0:T(8,128)}, f32[2,512,2304]{2,1,0:T(8,128)}) custom-call(f32[4]{0:T(128)} %pad_maximum_fusion.7.scalars_ref, f32[3,512,2304]{2,1,0:T(8,128)} %refs_0_.2, f32[512,2304]{1,0:T(8,128)} %get-tuple-element.195.refs_1_), custom_call_target="tpu_custom_call" | custom-call | flops 900000000 | tf_op jit(solution)/shard_map/optimizer/pallas_call | solution.py:738
  (265 shorter events, 167.3 us)
Async XLA Ops:
  7.2 349.5 %all-gather.2.cloned.1.call-start = ((), (), s32[]{:S(2)}) async-start(), calls=%async_computation | async-start | bytes 3342336 | tf_op jit(solution)/shard_map/all_gather | solution.py:1130
  8.3 25.6 %collective-permute-start.5 = (bf16[48,1152]{1,0:T(8,128)(2,1)S(1)}, bf16[48,1152]{1,0:T(8,128)(2,1)S(1)}, u32[]{:S(2)}, u32[]{:S(2)}) collective-permute-start(bf16[48,1152]{1,0:T(8,128)(2,1)S(1)} %fusion.2), channel_id=1, source_target_pairs={{0,8},{2,10},{4,12},{6,14},{8,0},{10,2},{12,4},{14,6},{16,24},{18,... | collective-permute-start | bytes 331784 | tf_op jit(solution)/shard_map/ppermute | solution.py:773
  11.3 26.0 %collective-permute-start.6 = (bf16[48,1152]{1,0:T(8,128)(2,1)S(1)}, bf16[48,1152]{1,0:T(8,128)(2,1)S(1)}, u32[]{:S(2)}, u32[]{:S(2)}) collective-permute-start(bf16[48,1152]{1,0:T(8,128)(2,1)S(1)} %fusion.2), channel_id=1, source_target_pairs={{0,16},{2,18},{4,20},{6,22},{8,24},{10,26},{12,28},{14,30},{16,0},... | collective-permute-start | bytes 331784 | tf_op jit(solution)/shard_map/ppermute | solution.py:773
  13.9 23.4 %collective-permute-start.7 = (bf16[48,1152]{1,0:T(8,128)(2,1)S(1)}, bf16[48,1152]{1,0:T(8,128)(2,1)S(1)}, u32[]{:S(2)}, u32[]{:S(2)}) collective-permute-start(bf16[48,1152]{1,0:T(8,128)(2,1)S(1)} %fusion.2), channel_id=1, source_target_pairs={{0,24},{2,26},{4,28},{6,30},{8,16},{10,18},{12,20},{14,22},{16,8},... | collective-permute-start | bytes 331784 | tf_op jit(solution)/shard_map/ppermute | solution.py:773
  33.8 26.4 %collective-permute-start.3 = (bf16[48,3456]{1,0:T(8,128)(2,1)S(1)}, bf16[48,3456]{1,0:T(8,128)(2,1)S(1)}, u32[]{:S(2)}, u32[]{:S(2)}) collective-permute-start(bf16[48,3456]{1,0:T(8,128)(2,1)S(1)} %constant_dynamic-update-slice_fusion), channel_id=1, source_target_pairs={{0,16},{2,18},{4,20},{6,22},{8,24},{10,26},{12,28},{14,30},{16,0},... | collective-permute-start | bytes 995336 | tf_op jit(solution)/shard_map/ppermute | solution.py:773
  37.3 22.9 %collective-permute-start.4 = (bf16[48,3456]{1,0:T(8,128)(2,1)S(1)}, bf16[48,3456]{1,0:T(8,128)(2,1)S(1)}, u32[]{:S(2)}, u32[]{:S(2)}) collective-permute-start(bf16[48,3456]{1,0:T(8,128)(2,1)S(1)} %constant_dynamic-update-slice_fusion), channel_id=1, source_target_pairs={{0,24},{2,26},{4,28},{6,30},{8,16},{10,18},{12,20},{14,22},{16,8},... | collective-permute-start | bytes 995336 | tf_op jit(solution)/shard_map/ppermute | solution.py:773
  37.4 22.8 %collective-permute-start.8 = (bf16[4,48,1152]{2,1,0:T(8,128)(2,1)S(1)}, bf16[4,48,1152]{2,1,0:T(8,128)(2,1)S(1)}, u32[]{:S(2)}, u32[]{:S(2)}) collective-permute-start(bf16[4,48,1152]{2,1,0:T(8,128)(2,1)S(1)} %pad_maximum_fusion.3.refs_1_), channel_id=1, source_target_pairs={{0,4},{2,6},{4,0},{6,2},{8,12},{10,14},{12,8},{14,10},{16,20},{18,... | collective-permute-start | bytes 1327112 | tf_op jit(solution)/shard_map/ppermute | solution.py:764
  39.2 21.1 %collective-permute-start.9 = (bf16[4,48,1152]{2,1,0:T(8,128)(2,1)S(1)}, bf16[4,48,1152]{2,1,0:T(8,128)(2,1)}, u32[]{:S(2)}, u32[]{:S(2)}) collective-permute-start(bf16[4,48,1152]{2,1,0:T(8,128)(2,1)S(1)} %pad_maximum_fusion.3.refs_1_), channel_id=1, source_target_pairs={{0,1},{1,0},{2,3},{3,2},{4,5},{5,4},{6,7},{7,6},{8,9},{9,8},{10,11... | collective-permute-start | bytes 1327112 | tf_op jit(solution)/shard_map/ppermute | solution.py:767
  72.4 38.9 %collective-permute-start.12 = (bf16[4,48,3456]{2,1,0:T(8,128)(2,1)}, bf16[4,48,3456]{2,1,0:T(8,128)(2,1)S(1)}, u32[]{:S(2)}, u32[]{:S(2)}) collective-permute-start(bf16[4,48,3456]{2,1,0:T(8,128)(2,1)} %pad_maximum_fusion.refs_3_.refs_1_), channel_id=1, source_target_pairs={{0,4},{2,6},{4,0},{6,2},{8,12},{10,14},{12,8},{14,10},{16,20},{18,... | collective-permute-start | bytes 3981320 | tf_op jit(solution)/shard_map/ppermute | solution.py:764
  73.9 37.5 %collective-permute-start.13 = (bf16[4,48,3456]{2,1,0:T(8,128)(2,1)}, bf16[4,48,3456]{2,1,0:T(8,128)(2,1)S(1)}, u32[]{:S(2)}, u32[]{:S(2)}) collective-permute-start(bf16[4,48,3456]{2,1,0:T(8,128)(2,1)} %pad_maximum_fusion.refs_3_.refs_1_), channel_id=1, source_target_pairs={{0,1},{1,0},{2,3},{3,2},{4,5},{5,4},{6,7},{7,6},{8,9},{9,8},{10,11... | collective-permute-start | bytes 3981320 | tf_op jit(solution)/shard_map/ppermute | solution.py:767
  111.4 17.3 %collective-permute-start.18 = (bf16[2,48,3456]{2,1,0:T(8,128)(2,1)S(1)}, bf16[2,48,3456]{2,1,0:T(8,128)(2,1)S(1)}, u32[]{:S(2)}, u32[]{:S(2)}) collective-permute-start(bf16[2,48,3456]{2,1,0:T(8,128)(2,1)S(1)} %slice.77), channel_id=1, source_target_pairs={{0,1},{1,0},{2,3},{3,2},{4,5},{5,4},{6,7},{7,6},{8,9},{9,8},{10,11... | collective-permute-start | bytes 1990664 | tf_op jit(solution)/shard_map/ppermute | solution.py:767
  113.7 18.7 %collective-permute-start.20 = (bf16[4,48,3456]{2,1,0:T(8,128)(2,1)}, bf16[4,48,3456]{2,1,0:T(8,128)(2,1)}, u32[]{:S(2)}, u32[]{:S(2)}) collective-permute-start(bf16[4,48,3456]{2,1,0:T(8,128)(2,1)} %pad_maximum_fusion.refs_3_.refs_1_), channel_id=1, source_target_pairs={{0,2},{2,0},{4,6},{6,4},{8,10},{10,8},{12,14},{14,12},{16,18},{18,... | collective-permute-start | bytes 3981320 | tf_op jit(solution)/shard_map/ppermute | solution.py:761
  113.7 18.7 %collective-permute-start.21 = (bf16[4,48,3456]{2,1,0:T(8,128)(2,1)S(1)}, bf16[4,48,3456]{2,1,0:T(8,128)(2,1)}, u32[]{:S(2)}, u32[]{:S(2)}) collective-permute-start(bf16[4,48,3456]{2,1,0:T(8,128)(2,1)S(1)} %collective-permute-done.12.refs_2_), channel_id=1, source_target_pairs={{0,2},{2,0},{4,6},{6,4},{8,10},{10,8},{12,14},{14,12},{16,18},{18,... | collective-permute-start | bytes 3981320 | tf_op jit(solution)/shard_map/ppermute | solution.py:761
  114.2 18.2 %collective-permute-start.22 = (bf16[4,48,3456]{2,1,0:T(8,128)(2,1)S(1)}, bf16[4,48,3456]{2,1,0:T(8,128)(2,1)}, u32[]{:S(2)}, u32[]{:S(2)}) collective-permute-start(bf16[4,48,3456]{2,1,0:T(8,128)(2,1)S(1)} %collective-permute-done.13.refs_3_), channel_id=1, source_target_pairs={{0,2},{2,0},{4,6},{6,4},{8,10},{10,8},{12,14},{14,12},{16,18},{18,... | collective-permute-start | bytes 3981320 | tf_op jit(solution)/shard_map/ppermute | solution.py:761
  210.5 39.8 %collective-permute-start.30 = (bf16[2,2,48,3456]{3,2,1,0:T(8,128)(2,1)}, bf16[2,2,48,3456]{3,2,1,0:T(8,128)(2,1)S(1)}, u32[]{:S(2)}, u32[]{:S(2)}) collective-permute-start(bf16[2,2,48,3456]{3,2,1,0:T(8,128)(2,1)} %get-tuple-element.148.refs_6_), channel_id=1, source_target_pairs={{0,4},{2,6},{4,0},{6,2},{8,12},{10,14},{12,8},{14,10},{16,20},{18,... | collective-permute-start | bytes 3981320 | tf_op jit(solution)/shard_map/ppermute | solution.py:764
  211.1 39.3 %collective-permute-start.31 = (bf16[4,48,3456]{2,1,0:T(8,128)(2,1)}, bf16[4,48,3456]{2,1,0:T(8,128)(2,1)S(1)}, u32[]{:S(2)}, u32[]{:S(2)}) collective-permute-start(bf16[4,48,3456]{2,1,0:T(8,128)(2,1)} %get-tuple-element.149.refs_7_), channel_id=1, source_target_pairs={{0,1},{1,0},{2,3},{3,2},{4,5},{5,4},{6,7},{7,6},{8,9},{9,8},{10,11... | collective-permute-start | bytes 3981320 | tf_op jit(solution)/shard_map/ppermute | solution.py:767
  266.9 22.0 %collective-permute-start.32 = (bf16[8,48,2304]{2,1,0:T(8,128)(2,1)S(1)}, bf16[8,48,2304]{2,1,0:T(8,128)(2,1)S(1)}, u32[]{:S(2)}, u32[]{:S(2)}) collective-permute-start(bf16[8,48,2304]{2,1,0:T(8,128)(2,1)S(1)} %dynamic-slice_bitcast_fusion.2), channel_id=1, source_target_pairs={{0,2},{2,0},{4,6},{6,4},{8,10},{10,8},{12,14},{14,12},{16,18},{18,... | collective-permute-start | bytes 5308424 | tf_op jit(solution)/shard_map/ppermute | solution.py:761
  266.9 17.3 %collective-permute-start.34 = (bf16[2,48,3456]{2,1,0:T(8,128)(2,1)S(1)}, bf16[2,48,3456]{2,1,0:T(8,128)(2,1)S(1)}, u32[]{:S(2)}, u32[]{:S(2)}) collective-permute-start(bf16[2,48,3456]{2,1,0:T(8,128)(2,1)S(1)} %copy-done.16), channel_id=1, source_target_pairs={{0,1},{1,0},{2,3},{3,2},{4,5},{5,4},{6,7},{7,6},{8,9},{9,8},{10,11... | collective-permute-start | bytes 1990664 | tf_op jit(solution)/shard_map/ppermute | solution.py:767
  316.7 36.1 %collective-permute-start.41 = (bf16[16,32,768]{2,1,0:T(8,128)(2,1)S(1)}, bf16[16,32,768]{2,1,0:T(8,128)(2,1)S(1)}, u32[]{:S(2)}, u32[]{:S(2)}) collective-permute-start(bf16[16,32,768]{2,1,0:T(8,128)(2,1)S(1)} %pad_maximum_fusion.1), channel_id=1, source_target_pairs={{0,2},{2,0},{4,6},{6,4},{8,10},{10,8},{12,14},{14,12},{16,18},{18,... | collective-permute-start | bytes 2359304 | tf_op jit(solution)/shard_map/ppermute | solution.py:761
  318.8 19.2 %collective-permute-start.47 = (bf16[48,3456]{1,0:T(8,128)(2,1)S(1)}, bf16[48,3456]{1,0:T(8,128)(2,1)S(1)}, u32[]{:S(2)}, u32[]{:S(2)}) collective-permute-start(bf16[48,3456]{1,0:T(8,128)(2,1)S(1)} %copy-done.27), channel_id=1, source_target_pairs={{0,8},{2,10},{4,12},{6,14},{8,0},{10,2},{12,4},{14,6},{16,24},{18,... | collective-permute-start | bytes 995336 | tf_op jit(solution)/shard_map/ppermute | solution.py:773
  321.2 25.8 %collective-permute-start.48 = (bf16[48,3456]{1,0:T(8,128)(2,1)S(1)}, bf16[48,3456]{1,0:T(8,128)(2,1)S(1)}, u32[]{:S(2)}, u32[]{:S(2)}) collective-permute-start(bf16[48,3456]{1,0:T(8,128)(2,1)S(1)} %copy-done.26), channel_id=1, source_target_pairs={{0,16},{2,18},{4,20},{6,22},{8,24},{10,26},{12,28},{14,30},{16,0},... | collective-permute-start | bytes 995336 | tf_op jit(solution)/shard_map/ppermute | solution.py:773
  322.2 27.6 %collective-permute-start.49 = (bf16[48,3456]{1,0:T(8,128)(2,1)S(1)}, bf16[48,3456]{1,0:T(8,128)(2,1)S(1)}, u32[]{:S(2)}, u32[]{:S(2)}) collective-permute-start(bf16[48,3456]{1,0:T(8,128)(2,1)S(1)} %copy-done.25), channel_id=1, source_target_pairs={{0,24},{2,26},{4,28},{6,30},{8,16},{10,18},{12,20},{14,22},{16,8},... | collective-permute-start | bytes 995336 | tf_op jit(solution)/shard_map/ppermute | solution.py:773
  335.5 28.4 %collective-permute-start.44 = (bf16[48,1280]{1,0:T(8,128)(2,1)}, bf16[48,1280]{1,0:T(8,128)(2,1)S(1)}, u32[]{:S(2)}, u32[]{:S(2)}) collective-permute-start(bf16[48,1280]{1,0:T(8,128)(2,1)} %get-tuple-element.179.refs_4_), channel_id=1, source_target_pairs={{0,8},{2,10},{4,12},{6,14},{8,0},{10,2},{12,4},{14,6},{16,24},{18,... | collective-permute-start | bytes 368648 | tf_op jit(solution)/shard_map/ppermute | solution.py:773
  338.0 25.9 %collective-permute-start.45 = (bf16[48,1280]{1,0:T(8,128)(2,1)}, bf16[48,1280]{1,0:T(8,128)(2,1)S(1)}, u32[]{:S(2)}, u32[]{:S(2)}) collective-permute-start(bf16[48,1280]{1,0:T(8,128)(2,1)} %get-tuple-element.180.refs_5_), channel_id=1, source_target_pairs={{0,16},{2,18},{4,20},{6,22},{8,24},{10,26},{12,28},{14,30},{16,0},... | collective-permute-start | bytes 368648 | tf_op jit(solution)/shard_map/ppermute | solution.py:773
  (78 other events, 554.8 us)
Sparse Core Ops, SparseCore 0:
  188.5 53.6 all-gather.1
